TPU v7x, 32 devices: a whole 2x2x4 slice. The times are simulated.
32 devices in a mesh: cfg: 2 (over x), space: 16 (over z, y, core).
Axes of the slice: x: 2, y: 2, z: 4, core: 2. Of those that a mesh axis runs over, the one named last changes fastest.
Arguments:
- eigenvectors: bfloat16 [8, 2, 3, 128, 16, 1024], P('cfg', None, None, None, 'space'), parts along dimension 0, may hold values from -3 to 3
- link_field: bfloat16 [8, 3, 2, 3, 3, 16, 1024], P('cfg', None, None, None, None, 'space'), parts along dimension 0, may hold values from -2.5 to 2.5
- momentum: int32 [3], replicated, may hold values from -2 to 2
- directions: int32 [4], replicated, may hold values from 0 to 2, as said below
- offsets: int32 [4], replicated, may hold values from 0 to 124
Outputs:
- elementals: float32 [8, 2, 4, 128, 128], P('cfg', None, None, 'space'), parts along dimension 0
There are 2 independent parts, one for each index of `cfg`. A program takes and returns all parts, laid end to end along the dimension named above; an argument that names none is the same for every part. Nothing has to cross between parts.
Inputs may be any that keep to these rules, and one draw needn't show every extreme that they name: `directions`: exactly 2 of the timeslices have direction 0 (the first dimension); each other one has direction 1 or 2.
All inputs are finite; a program needn't handle non-finite values.
Results may differ from a plain program's by a relative error of at most 0.0041.
Values may be sent and summed in bfloat16 or wider, within the bound.
A program may use at most 128 MiB of HBM per device.

v0:
```python
import math

import jax
import jax.numpy as jnp
from jax import lax
from jax.sharding import PartitionSpec as P

NEV = 128
BLK = 4
TSL = 4
LY = 32
LZ = 32


epsilon_cycles = ((0, 1, 2), (1, 2, 0), (2, 0, 1))


def from_behind(value, axis, steps):
    count = lax.axis_size(axis)
    pairs = [(source, (source + steps) % count) for source in range(count)]
    return lax.ppermute(value, axis, pairs)


def phase_table(momentum, x_sites, extent):
    y_sites = jnp.arange(LY, dtype=jnp.int32)
    z_sites = jnp.arange(LZ, dtype=jnp.int32)
    x_turns = (momentum[0] * x_sites % extent).astype(jnp.float32) / extent
    y_turns = (momentum[1] * y_sites % LY).astype(jnp.float32) / LY
    z_turns = (momentum[2] * z_sites % LZ).astype(jnp.float32) / LZ
    angles = (
        -2.0 * math.pi * (x_turns[:, None, None] + y_turns[None, :, None] + z_turns[None, None, :])
    )
    angles = angles.reshape(x_sites.shape[0], LY * LZ)
    return (jnp.cos(angles), jnp.sin(angles))


def roll_inner(field_in, axis_pos):
    leading_shape = field_in.shape[:-1]
    grid = field_in.reshape(leading_shape + (LY, LZ))
    grid = jnp.roll(grid, -1, axis=axis_pos)
    return grid.reshape(field_in.shape)


def along_first(vectors, above):
    return jnp.concatenate([vectors[:, :, :, 1:], above], axis=3)


def along_second(vectors, above):
    return roll_inner(vectors, -2)


def along_third(vectors, above):
    return roll_inner(vectors, -1)


def transport(link_now, source):
    link_re = link_now[0].astype(jnp.float32)
    link_im = link_now[1].astype(jnp.float32)
    src_re = source[0].astype(jnp.float32)
    src_im = source[1].astype(jnp.float32)
    rows_re = []
    rows_im = []
    for row in range(3):
        acc_re = link_re[row, 0] * src_re[0] - link_im[row, 0] * src_im[0]
        acc_im = link_re[row, 0] * src_im[0] + link_im[row, 0] * src_re[0]
        for column in range(1, 3):
            acc_re = (
                acc_re
                + link_re[row, column] * src_re[column]
                - link_im[row, column] * src_im[column]
            )
            acc_im = (
                acc_im
                + link_re[row, column] * src_im[column]
                + link_im[row, column] * src_re[column]
            )
        rows_re.append(acc_re)
        rows_im.append(acc_im)
    return jnp.stack([jnp.stack(rows_re), jnp.stack(rows_im)]).astype(jnp.bfloat16)


def pair_products(leading, partner, cosine, sine_values):
    lead_re = leading[0].astype(jnp.float32)
    lead_im = leading[1].astype(jnp.float32)
    part_re = partner[0].astype(jnp.float32)
    part_im = partner[1].astype(jnp.float32)
    layers = [None, None, None]
    for one_color, two_color, out_color in epsilon_cycles:
        prod_re = (
            lead_re[one_color][:, None] * part_re[two_color][None]
            - lead_im[one_color][:, None] * part_im[two_color][None]
            - lead_re[two_color][:, None] * part_re[one_color][None]
            + lead_im[two_color][:, None] * part_im[one_color][None]
        )
        prod_im = (
            lead_re[one_color][:, None] * part_im[two_color][None]
            + lead_im[one_color][:, None] * part_re[two_color][None]
            - lead_re[two_color][:, None] * part_im[one_color][None]
            - lead_im[two_color][:, None] * part_re[one_color][None]
        )
        layers[out_color] = (
            prod_re * cosine - prod_im * sine_values,
            prod_re * sine_values + prod_im * cosine,
        )
    real_part = jnp.stack([layers[0][0], layers[1][0], layers[2][0]])
    imag_part = jnp.stack([layers[0][1], layers[1][1], layers[2][1]])
    return jnp.stack([real_part, imag_part]).astype(jnp.bfloat16)


def contract(products, vectors):
    flat_products = products.reshape(products.shape[:4] + (-1,))
    flat_vectors = vectors.reshape(vectors.shape[:3] + (-1,))
    blocks = jnp.einsum(
        "rkabs,qkcs->brqac", flat_products, flat_vectors, preferred_element_type=jnp.float32
    )
    return jnp.stack([blocks[:, 0, 0] - blocks[:, 1, 1], blocks[:, 0, 1] + blocks[:, 1, 0]], axis=1)


def on_device(eigenvectors, link_field, momentum, directions, offsets):
    devices = lax.axis_size("space")
    planes = eigenvectors.shape[4]
    extent_x = planes * devices
    norm_factor = 1.0 / math.sqrt(extent_x * LY * LZ)
    x_sites = lax.axis_index("space") * planes + jnp.arange(planes, dtype=jnp.int32)
    cos_all, sin_all = phase_table(momentum, x_sites, extent_x)
    partial_list = []
    for tslice in range(TSL):
        vectors = eigenvectors[tslice]
        above = from_behind(eigenvectors[tslice], "space", -1)
        direction = directions[tslice]
        source = lax.switch(direction, [along_first, along_second, along_third], vectors, above)
        link_now = lax.dynamic_index_in_dim(link_field[tslice], direction, 0, keepdims=False)
        displaced = transport(link_now, source)
        leading = lax.dynamic_slice_in_dim(vectors, offsets[tslice], BLK, axis=2)
        products = pair_products(leading, displaced, cos_all, sin_all)

        def partial_term(first_row, row_count, products=products, vectors=vectors):
            chosen_rows = lax.dynamic_slice_in_dim(products, first_row, row_count, axis=3)
            return contract(chosen_rows, vectors) * norm_factor

        partial_list.append(partial_term(0, NEV))
    stacked = jnp.stack(partial_list)
    own_rows = lax.psum_scatter(stacked, "space", scatter_dimension=1, tiled=True)
    return jnp.transpose(own_rows, (0, 2, 3, 1, 4))


def solution(mesh):
    placed = (
        P("cfg", None, None, None, "space", None),
        P("cfg", None, None, None, None, "space", None),
        P(),
        P(),
        P(),
    )
    return jax.shard_map(
        on_device,
        mesh=mesh,
        in_specs=placed,
        out_specs=P("cfg", None, None, "space", None),
        check_vma=False,
    )
```

profile of v0, /device:TPU:0, one launch (start us, length us, event | category | flops | bytes accessed | tf_op | source)
XLA Modules:
  0.0 275.4 jit_solution(3868169293439341333)
XLA Ops:
  6.5 5.9 %slice_bitcast_fusion.77 = (bf16[2,3,128,1,1024]{4,2,1,0,3:T(8,128)(2,1)}, bf16[2,3,128,1,1024]{4,2,1,0,3:T(8,128)(2,1)}, bf16[2,3,128,1,1024]{4,2,1,0,3:T(8,128...) fusion(bf16[4,2,3,128,1,1024]{5,3,2,1,4,0:T(8,128)(2,1)} %bitca, ...), kind=kLoop, calls=%fused_computation.315 | loop fusion | bytes 18874368 | tf_op jit(solution)/shard_map/squeeze | solution.py:128
  12.4 5.4 %collective-permute-start = (bf16[2,3,128,1,1024]{4,2,1,0,3:T(8,128)(2,1)}, bf16[2,3,128,1,1024]{4,2,1,0,3:T(8,128)(2,1)}, u32[]{:S(2)}, u32[]{:S(2)}) collective-permute-start(bf16[2,3,128,1,1024]{4,2,1,0,3:T(8,128)(2,1)} %get-tuple-element.621), channel_id=1, source_target_pairs={{0,15},{1,0},{2,1},{3,2},{4,3},{5,4},{6,5},{7,6},{8,7},{9,8},{10,9... | collective-permute-start | bytes 4718600 | tf_op jit(solution)/shard_map/ppermute | solution.py:21
  54.8 7.1 %conditional.4 = (f32[1,128,1,1024]{1,3,2,0:T(8,128)S(1)}, f32[1,128,1,1024]{1,3,2,0:T(8,128)S(1)}, f32[1,128,1,1024]{1,3,2,0:T(8,128)S(1)}, f32[1,128,1,1024]{1...) conditional(s32[]{:T(128)} %clamp.12, ...), branch_computations={%region_0.1_spmd.clone, %region_1.2_spmd.clone, %region_2.3_spmd.c... | conditional | flops 3145728 | bytes 23593036 | solution.py:131
  54.9 2.6 copy.104
  57.5 2.2 slice.2180
  64.0 2.8 %subtract_convert_fusion.23 = (bf16[1,128,1,1024]{1,3,2,0:T(8,128)(2,1)S(1)}, bf16[1,128,1,1024]{1,3,2,0:T(8,128)(2,1)}, bf16[1,128,1,1024]{1,3,2,0:T(8,128)(2,1)}, bf16[1,128,1,1024]{1,3,2,0:T(8,128)(2,1)S(1)}) fusion(f32[1,128,1,1024]{1,3,2,0:T(8,128)S(1)} %get-tuple-element.390, f32[1,128,1,1024]{1,3,2,0:T(8,128)S(1)} %get-tuple-element.387, ...), kind=kLoop, calls=%fused_computation.220 | loop fusion | flops 6291456 | bytes 4243456 | tf_op jit(solution)/shard_map/convert.109
  70.2 2.0 copy.49
  76.7 2.1 copy.48
  80.8 2.1 copy.52
  82.9 11.9 %conditional.5 = (f32[1,128,1,1024]{1,3,2,0:T(8,128)S(1)}, f32[1,128,1,1024]{1,3,2,0:T(8,128)S(1)}, f32[1,128,1,1024]{1,3,2,0:T(8,128)S(1)}, f32[1,128,1,1024]{1...) conditional(s32[]{:T(128)} %clamp.13, ...), branch_computations={%region_3.4_spmd.clone, %region_4.5_spmd.clone, %region_5.6_spmd.c... | conditional | flops 3145728 | bytes 23593036 | solution.py:131
  82.9 2.7 fusion.99
  85.7 2.3 copy.113
  88.0 2.4 convert_element_type.870
  90.4 2.3 copy.114
  100.9 6.0 %subtract_convert_fusion.11 = (bf16[1,4,128,1,1024]{4,2,0,1,3:T(8,128)(2,1)}, bf16[1,4,128,1,1024]{4,2,0,1,3:T(8,128)(2,1)}, bf16[1,4,128,1,1024]{4,2,0,1,3:T(8,...) fusion(f32[1024]{0:T(1024)S(1)} %get-tuple-element.848, ...), kind=kLoop, calls=%fused_computation.142 | loop fusion | flops 34603008 | bytes 9543680 | tf_op jit(solution)/shard_map/convert.99
  114.2 2.1 copy.60
  118.4 2.1 copy.64
  120.4 2.3 maximum_bitcast_fusion.8
  123.6 3.2 %fusion.49 = f32[128,2,2,4,128]{4,0,2,3,1:T(8,128)S(1)} fusion(bf16[1,3,4,128,1024]{4,3,1,2,0:T(8,128)(2,1)S(1)} %maximum_bitcast_fusion.9, bf16[1,3,4,128,1024]{4,3,1,2,0:T(8,128)(2,1)S(1)} %maximum_bitcast_fusion.8, bf16[4,2,3,128,1,1024]{5,3,2,1,4,0:T(8,128)(2,1)} %bitcast.517), kind=kOutput, calls=%fused_computation.152 | convolution fusion | flops 1623195648 | bytes 8912896 | tf_op jit(solution)/shard_map/rkabs,qkcs->brqac/dot_general | solution.py:113
  128.3 20.2 %conditional.6 = (f32[1,128,1,1024]{1,3,2,0:T(8,128)}, f32[1,128,1,1024]{1,3,2,0:T(8,128)}, f32[1,128,1,1024]{1,3,2,0:T(8,128)}, f32[1,128,1,1024]{1,3,2,0:T(8,1...) conditional(s32[]{:T(128)} %clamp.14, ...), branch_computations={%region_6.7_spmd.clone, %region_7.8_spmd.clone, %region_8.9_spmd.c... | conditional | flops 3145728 | bytes 17301552 | solution.py:131
  128.3 2.5 fusion.104
  133.3 2.4 copy.116
  148.6 2.4 subtract_convert_fusion.16
  151.2 4.7 %subtract_convert_fusion.17 = (bf16[1,128,1,1024]{1,3,2,0:T(8,128)(2,1)S(1)}, bf16[1,128,1,1024]{1,3,2,0:T(8,128)(2,1)}, bf16[1,128,1,1024]{1,3,2,0:T(8,128)(2,1)}, bf16[1,128,1,1024]{1,3,2,0:T(8,128)(2,1)S(1)}) fusion(f32[1,128,1,1024]{1,3,2,0:T(8,128)} %get-tuple-element.402, f32[1,128,1,1024]{1,3,2,0:T(8,128)} %get-tuple-element.399, ...), kind=kLoop, calls=%fused_computation.208 | loop fusion | flops 6291456 | bytes 4243456 | tf_op jit(solution)/shard_map/convert.69
  161.7 5.7 %subtract_convert_fusion.8 = (bf16[1,4,128,1,1024]{4,2,0,1,3:T(8,128)(2,1)S(1)}, bf16[1,4,128,1,1024]{4,2,0,1,3:T(8,128)(2,1)S(1)}, bf16[1,4,128,1,1024]{4,2,0,1...) fusion(f32[128,1024]{1,0:T(8,128)} %copy.62, ...), kind=kLoop, calls=%fused_computation.130 | loop fusion | flops 34603008 | bytes 9543680 | tf_op jit(solution)/shard_map/convert.79
  169.6 4.4 %subtract_convert_fusion.5 = (bf16[1,4,128,1,1024]{4,2,0,1,3:T(8,128)(2,1)S(1)}, bf16[1,4,128,1,1024]{4,2,0,1,3:T(8,128)(2,1)S(1)}, bf16[1,4,128,1,1024]{4,2,0,1...) fusion(f32[128,1024]{1,0:T(8,128)S(1)} %copy-done.16, ...), kind=kLoop, calls=%fused_computation.118 | loop fusion | flops 34603008 | bytes 9543680 | tf_op jit(solution)/shard_map/convert.59
  181.1 3.3 %conditional.7 = (f32[1,128,1,1024]{1,3,2,0:T(8,128)}, f32[1,128,1,1024]{1,3,2,0:T(8,128)}, f32[1,128,1,1024]{1,3,2,0:T(8,128)}, f32[1,128,1,1024]{1,3,2,0:T(8,1...) conditional(s32[]{:T(128)} %clamp.15, ...), branch_computations={%region_9.10_spmd.clone, %region_10.11_spmd.clone, %region_11.12_s... | conditional | flops 3145728 | bytes 17301552 | solution.py:131
  184.5 2.5 subtract_convert_fusion.13
  187.1 4.7 %subtract_convert_fusion.14 = (bf16[1,128,1,1024]{1,3,2,0:T(8,128)(2,1)S(1)}, bf16[1,128,1,1024]{1,3,2,0:T(8,128)(2,1)}, bf16[1,128,1,1024]{1,3,2,0:T(8,128)(2,1)}, bf16[1,128,1,1024]{1,3,2,0:T(8,128)(2,1)S(1)}) fusion(f32[1,128,1,1024]{1,3,2,0:T(8,128)} %get-tuple-element.408, f32[1,128,1,1024]{1,3,2,0:T(8,128)} %get-tuple-element.405, ...), kind=kLoop, calls=%fused_computation.202 | loop fusion | flops 6291456 | bytes 4243456 | tf_op jit(solution)/shard_map/convert.49
  196.2 5.4 %subtract_convert_fusion.2 = (bf16[1,4,128,1,1024]{4,2,0,1,3:T(8,128)(2,1)S(1)}, bf16[1,4,128,1,1024]{4,2,0,1,3:T(8,128)(2,1)S(1)}, bf16[1,4,128,1,1024]{4,2,0,1...) fusion(f32[128,1024]{1,0:T(8,128)} %copy.84, ...), kind=kLoop, calls=%fused_computation.106 | loop fusion | flops 34603008 | bytes 9543680 | tf_op jit(solution)/shard_map/convert.39
  202.3 3.3 %fusion.40 = f32[128,2,2,4,128]{4,0,3,2,1:T(8,128)S(1)} fusion(bf16[1,3,4,128,1024]{4,3,1,2,0:T(8,128)(2,1)S(1)} %maximum_bitcast_fusion.15, bf16[1,3,4,128,1024]{4,3,1,2,0:T(8,128)(2,1)S(1)} %maximum_bitcast_fusion.14, bf16[4,2,3,128,1,1024]{5,3,2,1,4,0:T(8,128)(2,1)} %bitcast.518), kind=kOutput, calls=%fused_computation.149 | convolution fusion | flops 1623195648 | bytes 8912896 | tf_op jit(solution)/shard_map/rkabs,qkcs->brqac/dot_general | solution.py:113
  208.5 59.9 %reduce-scatter.2.cloned.1.call-done = f32[4,8,2,4,128]{4,1,3,2,0:T(8,128)} async-done(((f32[4,128,2,4,128]{4,1,3,2,0:T(8,128)}), f32[4,8,2,4,128]{4,1,3,2,0:T(8,128)}) %reduce-scatter.2.cloned.1.call-update) | async-done | bytes 131088 | tf_op jit(solution)/shard_map/reduce_scatter | solution.py:143
  (319 shorter events, 83.7 us)
Async XLA Ops:
  6.5 261.8 %reduce-scatter.2.cloned.1.call-start = ((), (), s32[]{:S(2)}) async-start(), calls=%async_computation.1 | async-start | bytes 2228224 | tf_op jit(solution)/shard_map/reduce_scatter | solution.py:143
  6.5 12.6 %copy-start.100 = (s32[4]{0:T(128)S(1)}, s32[4]{0:T(128)}, u32[]{:S(2)}) copy-start(s32[4]{0:T(128)} %param.20) | copy-start | bytes 52
  6.5 15.6 %copy-start.102 = (s32[3]{0:T(128)S(1)}, s32[3]{0:T(128)}, u32[]{:S(2)}) copy-start(s32[3]{0:T(128)} %param.19) | copy-start | bytes 40
  6.5 16.9 %copy-start.101 = (s32[4]{0:T(128)S(1)}, s32[4]{0:T(128)}, u32[]{:S(2)}) copy-start(s32[4]{0:T(128)} %param.21) | copy-start | bytes 52
  12.4 42.4 %collective-permute-start = (bf16[2,3,128,1,1024]{4,2,1,0,3:T(8,128)(2,1)}, bf16[2,3,128,1,1024]{4,2,1,0,3:T(8,128)(2,1)}, u32[]{:S(2)}, u32[]{:S(2)}) collective-permute-start(bf16[2,3,128,1,1024]{4,2,1,0,3:T(8,128)(2,1)} %get-tuple-element.621), channel_id=1, source_target_pairs={{0,15},{1,0},{2,1},{3,2},{4,3},{5,4},{6,5},{7,6},{8,7},{9,8},{10,9... | collective-permute-start | bytes 4718600 | tf_op jit(solution)/shard_map/ppermute | solution.py:21
  17.9 65.0 %collective-permute-start.1 = (bf16[2,3,128,1,1024]{4,2,1,0,3:T(8,128)(2,1)}, bf16[2,3,128,1,1024]{4,2,1,0,3:T(8,128)(2,1)}, u32[]{:S(2)}, u32[]{:S(2)}) collective-permute-start(bf16[2,3,128,1,1024]{4,2,1,0,3:T(8,128)(2,1)} %get-tuple-element.622), channel_id=1, source_target_pairs={{0,15},{1,0},{2,1},{3,2},{4,3},{5,4},{6,5},{7,6},{8,7},{9,8},{10,9... | collective-permute-start | bytes 4718600 | tf_op jit(solution)/shard_map/ppermute | solution.py:21
  18.5 109.8 %collective-permute-start.2 = (bf16[2,3,128,1,1024]{4,2,1,0,3:T(8,128)(2,1)}, bf16[2,3,128,1,1024]{4,2,1,0,3:T(8,128)(2,1)}, u32[]{:S(2)}, u32[]{:S(2)}) collective-permute-start(bf16[2,3,128,1,1024]{4,2,1,0,3:T(8,128)(2,1)} %get-tuple-element.623), channel_id=1, source_target_pairs={{0,15},{1,0},{2,1},{3,2},{4,3},{5,4},{6,5},{7,6},{8,7},{9,8},{10,9... | collective-permute-start | bytes 4718600 | tf_op jit(solution)/shard_map/ppermute | solution.py:21
  18.6 162.5 %collective-permute-start.3 = (bf16[2,3,128,1,1024]{4,2,1,0,3:T(8,128)(2,1)}, bf16[2,3,128,1,1024]{4,2,1,0,3:T(8,128)(2,1)}, u32[]{:S(2)}, u32[]{:S(2)}) collective-permute-start(bf16[2,3,128,1,1024]{4,2,1,0,3:T(8,128)(2,1)} %get-tuple-element.624), channel_id=1, source_target_pairs={{0,15},{1,0},{2,1},{3,2},{4,3},{5,4},{6,5},{7,6},{8,7},{9,8},{10,9... | collective-permute-start | bytes 4718600 | tf_op jit(solution)/shard_map/ppermute | solution.py:21
  82.9 12.1 %copy-start.46 = (f32[1,1,1,1024]{3,2,1,0:T(1,128)S(1)}, f32[1,1,1,1024]{3,2,1,0:T(1,128)}, u32[]{:S(2)}) copy-start(f32[1,1,1,1024]{3,2,1,0:T(1,128)} %get-tuple-element.797) | copy-start | bytes 12292
  82.9 12.1 %copy-start.47 = (f32[1,1,1,1024]{3,2,1,0:T(1,128)S(1)}, f32[1,1,1,1024]{3,2,1,0:T(1,128)}, u32[]{:S(2)}) copy-start(f32[1,1,1,1024]{3,2,1,0:T(1,128)} %get-tuple-element.798) | copy-start | bytes 12292
  82.9 12.1 %copy-start.48 = (f32[1,1,1,1024]{3,2,1,0:T(1,128)S(1)}, f32[1,1,1,1024]{3,2,1,0:T(1,128)}, u32[]{:S(2)}) copy-start(f32[1,1,1,1024]{3,2,1,0:T(1,128)} %get-tuple-element.799) | copy-start | bytes 12292
  82.9 12.1 %copy-start.49 = (f32[1,1,1,1024]{3,2,1,0:T(1,128)S(1)}, f32[1,1,1,1024]{3,2,1,0:T(1,128)}, u32[]{:S(2)}) copy-start(f32[1,1,1,1024]{3,2,1,0:T(1,128)} %get-tuple-element.806) | copy-start | bytes 12292
  82.9 12.1 %copy-start.50 = (f32[1,1,1,1024]{3,2,1,0:T(1,128)S(1)}, f32[1,1,1,1024]{3,2,1,0:T(1,128)}, u32[]{:S(2)}) copy-start(f32[1,1,1,1024]{3,2,1,0:T(1,128)} %get-tuple-element.807) | copy-start | bytes 12292
  82.9 12.1 %copy-start.51 = (f32[1,1,1,1024]{3,2,1,0:T(1,128)S(1)}, f32[1,1,1,1024]{3,2,1,0:T(1,128)}, u32[]{:S(2)}) copy-start(f32[1,1,1,1024]{3,2,1,0:T(1,128)} %get-tuple-element.808) | copy-start | bytes 12292
  120.4 2.8 %copy-start.4 = (bf16[1,4,128,1,1024]{4,2,0,1,3:T(8,128)(2,1)S(1)}, bf16[1,4,128,1,1024]{4,2,0,1,3:T(8,128)(2,1)}, u32[]{:S(2)}) copy-start(bf16[1,4,128,1,1024]{4,2,0,1,3:T(8,128)(2,1)} %get-tuple-element.719) | copy-start | bytes 3145732
  169.5 5.2 %slice-start = ((s8[6291456]{0:T(1024)(128)(4,1)}), s8[4194304]{0:T(1024)(128)(4,1)S(1)}, s32[]{:S(2)}) async-start(s8[6291456]{0:T(1024)(128)(4,1)} %bitcast.519), calls=%async_computation.2 | async-start | bytes 8388608
  181.0 3.5 %copy-start.42 = (f32[1,1,1,1024]{3,2,1,0:T(1,128)S(1)}, f32[1,1,1,1024]{3,2,1,0:T(1,128)}, u32[]{:S(2)}) copy-start(f32[1,1,1,1024]{3,2,1,0:T(1,128)} %get-tuple-element.835) | copy-start | bytes 12292
  181.0 3.5 %copy-start.43 = (f32[1,1,1,1024]{3,2,1,0:T(1,128)S(1)}, f32[1,1,1,1024]{3,2,1,0:T(1,128)}, u32[]{:S(2)}) copy-start(f32[1,1,1,1024]{3,2,1,0:T(1,128)} %get-tuple-element.842) | copy-start | bytes 12292
  181.1 3.5 %copy-start.44 = (f32[1,1,1,1024]{3,2,1,0:T(1,128)S(1)}, f32[1,1,1,1024]{3,2,1,0:T(1,128)}, u32[]{:S(2)}) copy-start(f32[1,1,1,1024]{3,2,1,0:T(1,128)} %get-tuple-element.843) | copy-start | bytes 12292
  181.1 3.5 %copy-start.45 = (f32[1,1,1,1024]{3,2,1,0:T(1,128)S(1)}, f32[1,1,1,1024]{3,2,1,0:T(1,128)}, u32[]{:S(2)}) copy-start(f32[1,1,1,1024]{3,2,1,0:T(1,128)} %get-tuple-element.844) | copy-start | bytes 12292
  184.4 2.6 copy-start.52
  184.4 2.6 copy-start.53
  184.4 2.6 copy-start.54
  184.4 2.6 copy-start.55
  184.4 2.6 copy-start.56
  184.4 2.6 copy-start.57
  184.4 2.6 copy-start.58
  184.5 2.6 copy-start.59
  184.5 2.6 copy-start.60
  184.5 2.6 copy-start.61
  202.3 3.4 %copy-start.20 = (f32[1,128,1,4,128]{4,1,3,2,0:T(8,128)S(1)}, f32[1,128,1,4,128]{4,1,3,2,0:T(8,128)}, u32[]{:S(2)}) copy-start(f32[1,128,1,4,128]{4,1,3,2,0:T(8,128)} %fusion.66) | copy-start | bytes 786436
  202.3 3.4 %copy-start.21 = (f32[1,128,1,4,128]{4,1,3,2,0:T(8,128)S(1)}, f32[1,128,1,4,128]{4,1,3,2,0:T(8,128)}, u32[]{:S(2)}) copy-start(f32[1,128,1,4,128]{4,1,3,2,0:T(8,128)} %fusion.68) | copy-start | bytes 786436
  (77 other events, 145.6 us)
Sparse Core Ops, SparseCore 0:
  208.6 59.7 reduce-scatter.1
where the time goes:
time: 280 us; the launch traced here: 275 us
  local copies, waits for them, and re-layouts  87.8 us (31%)
  other arithmetic  67.7 us (24%)
  waiting for transfers between devices  59.9 us (21%)
  between operations  32.6 us (12%)
  loops' own time  10.4 us (4%)
  matrix products  10.2 us (4%)
  starting transfers between devices  6.74 us (2%)
    reduce_scatter x1, waiting for transfers between devices, on_device(): lax.psum_scatter(stacked, 'space', scatter_dimension=1, tiled=True)  59.9 us
    another operation x12, other arithmetic  43.8 us
    mul x12, local copies, waits for them, and re-layouts, pair_products(): lead_im[one_color][:, None] * part_im[two_color][None]  13.4 us
    mul x12, local copies, waits for them, and re-layouts, pair_products(): lead_re[one_color][:, None] * part_re[two_color][None]  13.1 us
    another operation x4, loops' own time, on_device(): lax.switch(direction, [along_first, along_second, along_third], vectors,...  10.4 us
    dot_general x4, matrix products, contract(): jnp.einsum('rkabs,qkcs->brqac', flat_products, flat_vectors, preferred_el...  10.2 us
    cond x6, local copies, waits for them, and re-layouts  8.54 us
    mul x8, local copies, waits for them, and re-layouts, pair_products(): lead_im[two_color][:, None] * part_im[one_color][None]  7.96 us
  transfers between devices with their start and end apart: 5, of which 1 were waited for; matrix products, arithmetic and copies ran while one was open for 47% of the time, Pallas kernels for 0%

commit v1 on v0

v1 whole, which is shorter than its diff:
```python
import functools
import math

import jax
import jax.numpy as jnp
from jax import lax
from jax.experimental import pallas as pl
from jax.experimental.pallas import tpu as pltpu
from jax.sharding import PartitionSpec as P

BLK = 4
LY = 32
LZ = 32
SITES = 256
ROWS = 16
CHUNKS = 2
MESH = pl.DeviceIdType.MESH

epsilon_cycles = ((0, 1, 2), (1, 2, 0), (2, 0, 1))


def phase_table(momentum, x_sites, extent):
    y_sites = jnp.arange(LY, dtype=jnp.int32)
    z_sites = jnp.arange(LZ, dtype=jnp.int32)
    x_turns = (momentum[0] * x_sites % extent).astype(jnp.float32) / extent
    y_turns = (momentum[1] * y_sites % LY).astype(jnp.float32) / LY
    z_turns = (momentum[2] * z_sites % LZ).astype(jnp.float32) / LZ
    angles = (
        -2.0 * math.pi * (x_turns[:, None, None] + y_turns[None, :, None] + z_turns[None, None, :])
    )
    angles = angles.reshape(x_sites.shape[0], LY * LZ)
    return (jnp.cos(angles), jnp.sin(angles))


def products_of(source_at, link_ref, lead_ref, prod_ref, count):
    def rows_step(step, carry):
        first = pl.multiple_of(step * ROWS, ROWS)
        src_re = [source_at(0, c, first) for c in range(3)]
        src_im = [source_at(1, c, first) for c in range(3)]
        part_re = []
        part_im = []
        for row in range(3):
            acc_re = None
            acc_im = None
            for column in range(3):
                link_re = link_ref[0, row * 3 + column][None]
                link_im = link_ref[0, 9 + row * 3 + column][None]
                now_re = link_re * src_re[column] - link_im * src_im[column]
                now_im = link_re * src_im[column] + link_im * src_re[column]
                acc_re = now_re if acc_re is None else acc_re + now_re
                acc_im = now_im if acc_im is None else acc_im + now_im
            part_re.append(acc_re.astype(jnp.bfloat16).astype(jnp.float32))
            part_im.append(acc_im.astype(jnp.bfloat16).astype(jnp.float32))
        for a in range(BLK):
            lead_re = [lead_ref[0, c * BLK + a][None] for c in range(3)]
            lead_im = [lead_ref[0, (3 + c) * BLK + a][None] for c in range(3)]
            for one, two, out in epsilon_cycles:
                prod_re = (
                    lead_re[one] * part_re[two]
                    - lead_im[one] * part_im[two]
                    - lead_re[two] * part_re[one]
                    + lead_im[two] * part_im[one]
                )
                prod_im = (
                    lead_re[one] * part_im[two]
                    + lead_im[one] * part_re[two]
                    - lead_re[two] * part_im[one]
                    - lead_im[two] * part_re[one]
                )
                where = pl.ds(out * SITES, SITES)
                at_re = pl.multiple_of(a * count + first, ROWS)
                at_im = pl.multiple_of((BLK + a) * count + first, ROWS)
                prod_ref[pl.ds(at_re, ROWS), where] = prod_re.astype(jnp.bfloat16)
                prod_ref[pl.ds(at_im, ROWS), where] = prod_im.astype(jnp.bfloat16)
        return carry

    lax.fori_loop(0, count // ROWS, rows_step, 0)


def add_sites(vectors_ref, prod_ref, acc_ref, step):
    nev = vectors_ref.shape[3]
    total = None
    for k in range(3):
        weights = vectors_ref[0, :, k].reshape(2 * nev, SITES)
        now = lax.dot_general(
            prod_ref[:, k * SITES : (k + 1) * SITES],
            weights,
            (((1,), (1,)), ((), ())),
            preferred_element_type=jnp.float32,
        )
        total = now if total is None else total + now

    @pl.when(step == 0)
    def _():
        acc_ref[...] = total

    @pl.when(step > 0)
    def _():
        acc_ref[...] += total


def write_out(acc_ref, out_ref, count, nev, norm_factor, lead_index):
    half = BLK * count
    for a in range(BLK):
        rows_re = acc_ref[a * count : (a + 1) * count]
        rows_im = acc_ref[half + a * count : half + (a + 1) * count]
        out_re = (rows_re[:, :nev] - rows_im[:, nev:]) * norm_factor
        out_im = (rows_re[:, nev:] + rows_im[:, :nev]) * norm_factor
        for g in range(count // 8):
            out_ref[lead_index + (g, a)] = out_re[g * 8 : g * 8 + 8]
            out_ref[lead_index + (g, BLK + a)] = out_im[g * 8 : g * 8 + 8]


def local_kernel(norm_factor, info, vec_ref, next_ref, link_ref, lead_ref, out_ref, src_ref, prod_ref, acc_ref):
    step = pl.program_id(1)
    nev = vec_ref.shape[3]
    direction = info[2 + pl.program_id(0)]
    lane = lax.broadcasted_iota(jnp.int32, (ROWS, SITES), 1)

    def shift(second):
        def rows_step(i, carry):
            rows = pl.ds(pl.multiple_of(i * ROWS, ROWS), ROWS)
            for r in range(2):
                for c in range(3):
                    now = vec_ref[0, r, c, rows].astype(jnp.float32)
                    if second:
                        after = next_ref[0, r, c, rows].astype(jnp.float32)
                        moved = jnp.where(
                            lane < SITES - LZ,
                            pltpu.roll(now, SITES - LZ, 1),
                            pltpu.roll(after, SITES - LZ, 1),
                        )
                    else:
                        moved = jnp.where(
                            lane % LZ == LZ - 1,
                            pltpu.roll(now, LZ - 1, 1),
                            pltpu.roll(now, SITES - 1, 1),
                        )
                    src_ref[r, c, rows] = moved
            return carry

        lax.fori_loop(0, nev // ROWS, rows_step, 0)

    @pl.when(direction == 1)
    def _():
        shift(True)

    @pl.when(direction != 1)
    def _():
        shift(False)

    products_of(lambda r, c, first: src_ref[r, c, pl.ds(first, ROWS)], link_ref, lead_ref, prod_ref, nev)
    add_sites(vec_ref, prod_ref, acc_ref, step)

    @pl.when(step == pl.num_programs(1) - 1)
    def _():
        write_out(acc_ref, out_ref, nev, nev, norm_factor, (0,))


def remote_kernel(norm_factor, info, vec_ref, src_ref, link_ref, lead_ref, out_ref, prod_ref, acc_ref):
    step = pl.program_id(0)
    nev = vec_ref.shape[3]
    count = src_ref.shape[2]
    products_of(
        lambda r, c, first: src_ref[r, c, pl.ds(first, ROWS)].astype(jnp.float32),
        link_ref, lead_ref, prod_ref, count,
    )
    add_sites(vec_ref, prod_ref, acc_ref, step)

    @pl.when(step == pl.num_programs(0) - 1)
    def _():
        write_out(acc_ref, out_ref, count, nev, norm_factor, ())


def local_sums(info, vectors, links, leads, norm_factor):
    slices, _, _, nev, sites = vectors.shape
    steps = sites // SITES
    count = slices // 2
    flops = count * 2 * 8 * nev * 3 * sites * 2 * nev
    return pl.pallas_call(
        functools.partial(local_kernel, norm_factor),
        out_shape=jax.ShapeDtypeStruct((count, nev // 8, 2 * BLK, 8, nev), jnp.float32),
        grid_spec=pltpu.PrefetchScalarGridSpec(
            num_scalar_prefetch=1,
            grid=(count, steps),
            in_specs=[
                pl.BlockSpec((1, 2, 3, nev, SITES), lambda t, s, info: (info[t], 0, 0, 0, s)),
                pl.BlockSpec((1, 2, 3, nev, SITES), lambda t, s, info: (info[t], 0, 0, 0, (s + 1) % steps)),
                pl.BlockSpec((1, 18, SITES), lambda t, s, info: (count + t, 0, s)),
                pl.BlockSpec((1, 6 * BLK, SITES), lambda t, s, info: (count + t, 0, s)),
            ],
            out_specs=pl.BlockSpec((1, nev // 8, 2 * BLK, 8, nev), lambda t, s, info: (t, 0, 0, 0, 0)),
            scratch_shapes=[
                pltpu.VMEM((2, 3, nev, SITES), jnp.float32),
                pltpu.VMEM((2 * BLK * nev, 3 * SITES), jnp.bfloat16),
                pltpu.VMEM((2 * BLK * nev, 2 * nev), jnp.float32),
            ],
        ),
        compiler_params=pltpu.CompilerParams(vmem_limit_bytes=40 * 2**20),
        cost_estimate=pl.CostEstimate(flops=flops, bytes_accessed=count * 4 * 2**20, transcendentals=0),
        name="local_sums",
    )(info, vectors, vectors, links, leads)


def remote_sums(info, vectors, source, links, leads, place, norm_factor):
    _, _, _, nev, sites = vectors.shape
    count = source.shape[2]
    steps = sites // SITES
    flops = 2 * 8 * count * 3 * sites * 2 * nev
    return pl.pallas_call(
        functools.partial(remote_kernel, norm_factor),
        out_shape=jax.ShapeDtypeStruct((count // 8, 2 * BLK, 8, nev), jnp.float32),
        grid_spec=pltpu.PrefetchScalarGridSpec(
            num_scalar_prefetch=1,
            grid=(steps,),
            in_specs=[
                pl.BlockSpec((1, 2, 3, nev, SITES), lambda s, info: (info[0], 0, 0, 0, s)),
                pl.BlockSpec((2, 3, count, SITES), lambda s, info: (0, 0, 0, s)),
                pl.BlockSpec((1, 18, SITES), lambda s, info: (place, 0, s)),
                pl.BlockSpec((1, 6 * BLK, SITES), lambda s, info: (place, 0, s)),
            ],
            out_specs=pl.BlockSpec((count // 8, 2 * BLK, 8, nev), lambda s, info: (0, 0, 0, 0)),
            scratch_shapes=[
                pltpu.VMEM((2 * BLK * count, 3 * SITES), jnp.bfloat16),
                pltpu.VMEM((2 * BLK * count, 2 * nev), jnp.float32),
            ],
        ),
        compiler_params=pltpu.CompilerParams(vmem_limit_bytes=40 * 2**20),
        cost_estimate=pl.CostEstimate(flops=flops, bytes_accessed=3 * 2**20, transcendentals=0),
        name="remote_sums",
    )(info, vectors, source, links, leads)


def scatter_kernel(groups, part_ref, out_ref, send_one, send_two, send_three, recv_one, recv_two, recv_three, sum_one, sum_two, sems_out, sems_in):
    me = lax.axis_index("space")
    core = me % 2
    row = (me // 2) % 2
    group = me // 4
    pair = me + 1 - 2 * core
    across = me + 2 - 4 * row
    others = [(group + step) % groups for step in range(1, groups)]
    barrier = pltpu.get_barrier_semaphore()
    for partner in [pair, across] + [other * 4 + row * 2 + core for other in others]:
        pl.semaphore_signal(barrier, inc=1, device_id={"space": partner}, device_id_type=MESH)
    pl.semaphore_wait(barrier, groups + 1)

    def copy(source, target, number, partner):
        return pltpu.make_async_remote_copy(
            src_ref=source, dst_ref=target, send_sem=sems_out.at[number], recv_sem=sems_in.at[number],
            device_id={"space": partner}, device_id_type=MESH,
        )

    for z in range(groups):
        for y in range(2):
            send_one[z, y] = part_ref[z, y, 1 - core].astype(jnp.bfloat16)
    first = copy(send_one, recv_one, 0, pair)
    first.start()
    first.wait()
    for z in range(groups):
        got = part_ref[z, 1 - row, core] + recv_one[z, 1 - row].astype(jnp.float32)
        send_two[z] = got.astype(jnp.bfloat16)
    second = copy(send_two, recv_two, 1, across)
    second.start()
    for z in range(groups):
        sum_one[z] = part_ref[z, row, core] + recv_one[z, row].astype(jnp.float32)
    second.wait()
    for z in range(groups):
        sum_two[z] = sum_one[z] + recv_two[z].astype(jnp.float32)
        send_three[z] = sum_two[z].astype(jnp.bfloat16)
    copies = []
    for step, other in enumerate(others):
        copies.append(copy(send_three.at[other], recv_three.at[step], 2 + step, other * 4 + row * 2 + core))
        copies[-1].start()
    total = sum_two[group]
    for step in range(groups - 1):
        copies[step].wait()
        total = total + recv_three[step].astype(jnp.float32)
    out_ref[...] = total


def scatter_sum(part, number):
    devices, rows, columns = part.shape
    groups = devices // 4
    whole = pl.BlockSpec(memory_space=pltpu.VMEM)
    bf16 = jnp.bfloat16
    return pl.pallas_call(
        functools.partial(scatter_kernel, groups),
        out_shape=jax.ShapeDtypeStruct((rows, columns), jnp.float32),
        in_specs=[whole],
        out_specs=whole,
        scratch_shapes=[
            pltpu.VMEM((groups, 2, rows, columns), bf16),
            pltpu.VMEM((groups, rows, columns), bf16),
            pltpu.VMEM((groups, rows, columns), bf16),
            pltpu.VMEM((groups, 2, rows, columns), bf16),
            pltpu.VMEM((groups, rows, columns), bf16),
            pltpu.VMEM((groups, rows, columns), bf16),
            pltpu.VMEM((groups, rows, columns), jnp.float32),
            pltpu.VMEM((groups, rows, columns), jnp.float32),
            pltpu.SemaphoreType.DMA((groups + 1,)),
            pltpu.SemaphoreType.DMA((groups + 1,)),
        ],
        compiler_params=pltpu.CompilerParams(
            collective_id=number, has_side_effects=True, vmem_limit_bytes=40 * 2**20
        ),
        name="scatter_sum",
    )(part.reshape(groups, 2, 2, rows, columns))


def by_owner(part, devices):
    slices, tiles, parts, eight, nev = part.shape
    own = tiles * eight // devices
    if own == eight:
        moved = jnp.transpose(part, (1, 0, 2, 3, 4))
    else:
        flat = jnp.transpose(part, (0, 2, 1, 3, 4)).reshape(slices, parts, devices, own, nev)
        moved = jnp.transpose(flat, (2, 0, 1, 3, 4))
    return moved.reshape(devices, slices * parts * own, nev)


def on_device(eigenvectors, link_field, momentum, directions, offsets):
    devices = lax.axis_size("space")
    slices, _, _, nev, planes, sites = eigenvectors.shape
    extent_x = planes * devices
    norm_factor = 1.0 / math.sqrt(extent_x * LY * LZ)
    x_sites = lax.axis_index("space") * planes + jnp.arange(planes, dtype=jnp.int32)
    vectors = eigenvectors.reshape(slices, 2, 3, nev, sites)

    inner = (directions != 0).astype(jnp.int32)
    numbers = jnp.arange(slices, dtype=jnp.int32)
    before = (inner[None] < inner[:, None]) | (
        (inner[None] == inner[:, None]) & (numbers[None] < numbers[:, None])
    )
    rank = jnp.sum(before.astype(jnp.int32), axis=1)
    order = [jnp.sum(jnp.where(rank == place, numbers, 0)) for place in range(slices)]
    half = slices // 2

    size = nev // CHUNKS
    pairs = [(source, (source - 1) % devices) for source in range(devices)]
    above = []
    for place in range(half):
        for chunk in range(CHUNKS):
            piece = lax.dynamic_slice(
                vectors, (order[place], 0, 0, chunk * size, 0), (1, 2, 3, size, sites)
            )
            above.append(lax.ppermute(piece, "space", pairs)[0])

    cosine, sine = phase_table(momentum, x_sites, extent_x)
    links = []
    leads = []
    for place in range(slices):
        now = order[place]
        link = lax.dynamic_slice(
            link_field, (now, directions[now], 0, 0, 0, 0, 0), (1, 1) + link_field.shape[2:]
        )
        links.append(link.reshape(18, sites).astype(jnp.float32))
        lead = lax.dynamic_slice(
            vectors, (now, 0, 0, offsets[now], 0), (1, 2, 3, BLK, sites)
        )[0].astype(jnp.float32)
        turned = jnp.stack([lead[0] * cosine - lead[1] * sine, lead[0] * sine + lead[1] * cosine])
        leads.append(turned.reshape(6 * BLK, sites))
    links = jnp.stack(links)
    leads = jnp.stack(leads)

    info = jnp.stack(order[half:] + [directions[now] for now in order[half:]])
    inner_part = local_sums(info, vectors, links, leads, norm_factor)
    inner_sum = scatter_sum(by_owner(inner_part, devices), 0)
    outer = []
    for place in range(half):
        pieces = [
            remote_sums(
                order[place][None], vectors, above[place * CHUNKS + chunk], links, leads, place, norm_factor
            )
            for chunk in range(CHUNKS)
        ]
        outer.append(jnp.concatenate(pieces))
    outer_sum = scatter_sum(by_owner(jnp.stack(outer), devices), 1)

    own = nev // devices
    both = jnp.concatenate([outer_sum, inner_sum]).reshape(slices, 2, BLK, own, nev)
    return jnp.take(both, rank, axis=0, mode="clip")


def solution(mesh):
    placed = (
        P("cfg", None, None, None, "space", None),
        P("cfg", None, None, None, None, "space", None),
        P(),
        P(),
        P(),
    )
    return jax.shard_map(
        on_device,
        mesh=mesh,
        in_specs=placed,
        out_specs=P("cfg", None, None, "space", None),
        check_vma=False,
    )
```

time: 280 us -> 127 us (0.45); the launches traced: 275 us -> 126 us
  local copies, waits for them, and re-layouts: 87.8 us -> 14.5 us
  Pallas kernels: 0 us -> 71.5 us
  waiting for transfers between devices: 59.9 us -> 0.01 us
  other arithmetic: 67.7 us -> 9.64 us
  loops' own time: 10.4 us -> 0 us
  matrix products: 10.2 us -> 0 us
  between operations: 32.6 us -> 23.5 us
    pallas_call x0 -> x7, Pallas kernels: none -> 71.5 us  [the longest x2 24.7 us: scatter_sum(): pl.pallas_call(functools.partial(scatter_kernel, groups), out_shape=jax.S...]
    reduce_scatter x1 -> x0, waiting for transfers between devices: 59.9 us -> none  [on_device(): lax.psum_scatter(stacked, 'space', scatter_dimension=1, tiled=True)]
    another operation x26 -> x8, other arithmetic: 53.3 us -> 3.66 us  [the longest x1 2.63 us: on_device(): info = jnp.stack(order[half:] + [directions[now] for now in order[half:]])]
    mul x40 -> x0, local copies, waits for them, and re-layouts: 41.6 us -> none  [the longest x12 13.4 us: pair_products(): lead_im[one_color][:, None] * part_im[two_color][None]]
    slice x23 -> x0, local copies, waits for them, and re-layouts: 24.8 us -> none  [the longest x2 5.22 us: transport(): src_im = source[1].astype(jnp.float32)]
    another operation x4 -> x0, loops' own time: 10.4 us -> none  [on_device(): lax.switch(direction, [along_first, along_second, along_third], vectors,...]
    dot_general x4 -> x0, matrix products: 10.2 us -> none  [contract(): jnp.einsum('rkabs,qkcs->brqac', flat_products, flat_vectors, preferred_el...]
    convert_element_type x18 -> x3, other arithmetic: 12.2 us -> 2.9 us  [the longest x2 2.17 us: on_device(): lead = lax.dynamic_slice(vectors, (now, 0, 0, offsets[now], 0), (1, 2, 3,...]
  transfers between devices with their start and end apart: 5 -> 4, of which waited for: 1 -> 0; matrix products, arithmetic and copies ran while one was open for 47% -> 12% of each run, Pallas kernels for 0% -> 43%
where the time goes in v1:
time: 127 us; the launch traced here: 126 us
  Pallas kernels  71.5 us (56%)
  between operations  23.5 us (19%)
  local copies, waits for them, and re-layouts  14.5 us (11%)
  other arithmetic  9.64 us (8%)
  starting transfers between devices  6.74 us (5%)
    pallas_call x2, Pallas kernels, scatter_sum(): pl.pallas_call(functools.partial(scatter_kernel, groups), out_shape=jax.S...  24.7 us
    pallas_call x1, Pallas kernels, local_sums(): pl.pallas_call(functools.partial(local_kernel, norm_factor), out_shape=ja...  23.4 us
    pallas_call x4, Pallas kernels, remote_sums(): pl.pallas_call(functools.partial(remote_kernel, norm_factor), out_shape=j...  23.4 us
    ppermute x4, starting transfers between devices, on_device(): above.append(lax.ppermute(piece, 'space', pairs)[0])  6.74 us
    unnamed x15, local copies, waits for them, and re-layouts  3.72 us
    dynamic_slice x1, local copies, waits for them, and re-layouts, on_device(): lax.dynamic_slice(vectors, (order[place], 0, 0, chunk * size, 0), (1, 2,...  3.65 us
    dynamic_slice x5, local copies, waits for them, and re-layouts, on_device(): lax.dynamic_slice(link_field, (now, directions[now], 0, 0, 0, 0, 0), (1,...  3.19 us
    another operation x1, other arithmetic, on_device(): info = jnp.stack(order[half:] + [directions[now] for now in order[half:]])  2.63 us
  transfers between devices with their start and end apart: 4, of which 0 were waited for; matrix products, arithmetic and copies ran while one was open for 12% of the time, Pallas kernels for 43%

profile of v1, /device:TPU:0, one launch (start us, length us, event | category | flops | bytes accessed | tf_op | source)
XLA Modules:
  0.0 125.9 jit_solution(6070567355228824847)
XLA Ops:
  0.0 0.7 compare_convert_fusion
  0.7 0.2 convert_reduce_fusion
  0.9 0.8 fusion.5
  5.4 3.6 %dynamic-slice_bitcast_fusion.3 = (bf16[1,2,3,64,1024]{4,3,2,1,0:T(8,128)(2,1)}, bf16[1,2,3,64,1024]{4,3,2,1,0:T(8,128)(2,1)}, bf16[1,2,3,64,1024]{4,3,2,1,0:T(8,128)(2,1)}, bf16[1,2,3,64,1024]{4,3,2,1,0:T(8,128)(2,1)}) fusion(bf16[4,2,3,128,1,1024]{5,3,4,2,1,0:T(8,128)(2,1)} %param.5, s32[]{:T(128)S(6)} %select_n.93, s32[]{:T(128)S(6)} %select_n.96), kind=kLoop, calls=%fused_computation.5 | loop fusion | bytes 6291464 | tf_op jit(solution)/shard_map/dynamic_slice | solution.py:343
  9.1 5.4 %collective-permute-start = (bf16[1,2,3,64,1024]{4,3,2,1,0:T(8,128)(2,1)}, bf16[1,2,3,64,1024]{4,3,2,1,0:T(8,128)(2,1)}, u32[]{:S(2)}, u32[]{:S(2)}) collective-permute-start(bf16[1,2,3,64,1024]{4,3,2,1,0:T(8,128)(2,1)} %get-tuple-element.9), channel_id=1, source_target_pairs={{0,15},{1,0},{2,1},{3,2},{4,3},{5,4},{6,5},{7,6},{8,7},{9,8},{10,9... | collective-permute-start | bytes 2359304 | tf_op jit(solution)/shard_map/ppermute | solution.py:346
  14.5 0.7 collective-permute-start.1
  15.2 0.6 collective-permute-start.3
  19.6 0.7 fusion.16
  23.9 0.7 fusion.17
  31.6 1.3 fusion.11
  32.8 0.1 broadcast_reduce_fusion
  33.8 0.9 dynamic-slice_convert_fusion
  36.6 1.2 dynamic-slice_convert_fusion.1
  37.8 0.7 multiply_subtract_fusion
  38.6 0.7 stack_reshape.13
  39.4 0.8 pad_maximum_fusion.4
  40.2 0.9 constant_dynamic-update-slice_fusion.2
  43.7 1.6 %constant_dynamic-slice_fusion.3 = (bf16[1,1,2,3,3,1,1024]{6,2,5,4,3,1,0:T(2,128)(2,1)}, bf16[1,1,2,3,3,1,1024]{6,2,5,4,3,1,0:T(2,128)(2,1)S(1)}, bf16[1,1,2,3,3...) fusion(bf16[4,3,2,3,3,1,1024]{6,2,5,4,3,1,0:T(2,128)(2,1)} %param.6, s32[]{:T(128)S(6)} %select_n.93, ...), kind=kLoop, calls=%fused_computation.45 | loop fusion | bytes 294944 | tf_op jit(solution)/shard_map/dynamic_slice | solution.py:353
  45.3 2.6 %pad_add_fusion.info = s32[4]{0:T(128)S(1)} fusion(s32[1]{0:T(128)} %get-tuple-element.52, s32[1]{0:T(128)} %get-tuple-element.51, s32[1]{0:T(128)} %bitcast.38, s32[1]{0:T(128)} %bitcast.37), kind=kLoop, calls=%fused_computation.74 | loop fusion | flops 12 | bytes 32 | tf_op jit(solution)/shard_map/stack | solution.py:365
  47.9 0.8 copy.26
  48.9 0.8 copy.29
  49.8 2.8 %copy-done = bf16[4,2,3,128,1,1024]{5,3,4,2,1,0:T(8,128)(2,1)S(1)} copy-done((bf16[4,2,3,128,1,1024]{5,3,4,2,1,0:T(8,128)(2,1)S(1)}, bf16[4,2,3,128,1,1024]{5,3,4,2,1,0:T(8,128)(2,1)}, u32[]{:S(2)}) %copy-start) | copy-done | bytes 6291480
  52.6 23.4 %local_sums.1 = f32[2,16,8,8,128]{4,3,2,1,0:T(8,128)S(1)} custom-call(s32[4]{0:T(128)S(1)} %pad_add_fusion.info, bf16[4,2,3,128,1024]{4,3,2,1,0:T(8,128)(2,1)S(1)} %bitcast.99, bf16[4,2,3,128,1024]{4,3,2,1,0:T(8,128)(2,1)S(1)} %bitcast.100, f32[4,18,1024]{2,1,0:T(8,128)S(1)} %maximum_convert_fusion.link_ref, ...), custom_call_target="tpu_custom_call" | custom-call | flops 3221225472 | bytes 8388608 | tf_op jit(solution)/shard_map/local_sums/pallas_call | solution.py:180
  76.2 12.9 %scatter_sum.3 = f32[128,128]{1,0:T(8,128)S(1)} custom-call(f32[4,2,2,128,128]{4,3,2,1,0:T(8,128)S(1)} %bitcast.108), custom_call_target="tpu_custom_call" | custom-call | tf_op jit(solution)/shard_map/scatter_sum/pallas_call | solution.py:286
  89.1 6.0 %remote_sums.4 = f32[8,8,8,128]{3,2,1,0:T(8,128)S(1)} custom-call(s32[1]{0:T(128)} %bitcast.info, bf16[4,2,3,128,1024]{4,3,2,1,0:T(8,128)(2,1)S(1)} %bitcast.103, bf16[2,3,64,1024]{3,2,1,0:T(8,128)(2,1)} %bitcast.3.src_ref, f32[4,18,1024]{2,1,0:T(8,128)S(1)} %maximum_convert_fusion.link_ref, f32[4,24,1024]{2,1,0:T(8,128)S(1)} %constant_dynamic-update-slice_fusion.lead_ref), custom_call_target="tpu_custom_call" | custom-call | flops 805306368 | bytes 3145728 | tf_op jit(solution)/shard_map/remote_sums/pallas_call | solution.py:210
  95.1 6.0 %remote_sums.5 = f32[8,8,8,128]{3,2,1,0:T(8,128)S(1)} custom-call(s32[1]{0:T(128)} %bitcast.info, bf16[4,2,3,128,1024]{4,3,2,1,0:T(8,128)(2,1)S(1)} %bitcast.104, bf16[2,3,64,1024]{3,2,1,0:T(8,128)(2,1)} %bitcast.27.src_ref, f32[4,18,1024]{2,1,0:T(8,128)S(1)} %maximum_convert_fusion.link_ref, f32[4,24,1024]{2,1,0:T(8,128)S(1)} %constant_dynamic-update-slice_fusion.lead_ref), custom_call_target="tpu_custom_call" | custom-call | flops 805306368 | bytes 3145728 | tf_op jit(solution)/shard_map/remote_sums/pallas_call | solution.py:210
  101.1 6.1 %remote_sums.6 = f32[8,8,8,128]{3,2,1,0:T(8,128)S(1)} custom-call(s32[1]{0:T(128)} %bitcast.29.info, bf16[4,2,3,128,1024]{4,3,2,1,0:T(8,128)(2,1)S(1)} %bitcast.105, bf16[2,3,64,1024]{3,2,1,0:T(8,128)(2,1)} %bitcast.31.src_ref, f32[4,18,1024]{2,1,0:T(8,128)S(1)} %maximum_convert_fusion.link_ref, f32[4,24,1024]{2,1,0:T(8,128)S(1)} %constant_dynamic-update-slice_fusion.lead_ref), custom_call_target="tpu_custom_call" | custom-call | flops 805306368 | bytes 3145728 | tf_op jit(solution)/shard_map/remote_sums/pallas_call | solution.py:210
  107.2 5.3 %remote_sums.7 = f32[8,8,8,128]{3,2,1,0:T(8,128)S(1)} custom-call(s32[1]{0:T(128)} %bitcast.29.info, bf16[4,2,3,128,1024]{4,3,2,1,0:T(8,128)(2,1)S(1)} %bitcast.106, bf16[2,3,64,1024]{3,2,1,0:T(8,128)(2,1)S(1)} %bitcast.110, f32[4,18,1024]{2,1,0:T(8,128)S(1)} %maximum_convert_fusion.link_ref, f32[4,24,1024]{2,1,0:T(8,128)S(1)} %constant_dynamic-update-slice_fusion.lead_ref), custom_call_target="tpu_custom_call" | custom-call | flops 805306368 | bytes 3145728 | tf_op jit(solution)/shard_map/remote_sums/pallas_call | solution.py:210
  112.6 0.1 maximum_bitcast_fusion
  112.7 0.1 copy.34
  112.8 11.9 %scatter_sum.2 = f32[128,128]{1,0:T(8,128)S(1)} custom-call(f32[4,2,2,128,128]{4,3,2,1,0:T(8,128)S(1)} %bitcast.109), custom_call_target="tpu_custom_call" | custom-call | tf_op jit(solution)/shard_map/scatter_sum/pallas_call | solution.py:286
  124.7 1.2 gather_fusion
  (42 shorter events, 0.9 us)
Async XLA Ops:
  0.0 19.6 %copy-start.2 = (s32[4]{0:T(128)S(1)}, s32[4]{0:T(128)}, u32[]{:S(2)}) copy-start(s32[4]{0:T(128)} %param.8) | copy-start | bytes 52
  0.0 19.6 %copy-start.1 = (s32[4]{0:T(128)S(1)}, s32[4]{0:T(128)}, u32[]{:S(2)}) copy-start(s32[4]{0:T(128)} %param.9) | copy-start | bytes 52
  0.0 23.9 %copy-start.3 = (s32[3]{0:T(128)S(1)}, s32[3]{0:T(128)}, u32[]{:S(2)}) copy-start(s32[3]{0:T(128)} %param.7) | copy-start | bytes 40
  9.1 80.0 %collective-permute-start = (bf16[1,2,3,64,1024]{4,3,2,1,0:T(8,128)(2,1)}, bf16[1,2,3,64,1024]{4,3,2,1,0:T(8,128)(2,1)}, u32[]{:S(2)}, u32[]{:S(2)}) collective-permute-start(bf16[1,2,3,64,1024]{4,3,2,1,0:T(8,128)(2,1)} %get-tuple-element.9), channel_id=1, source_target_pairs={{0,15},{1,0},{2,1},{3,2},{4,3},{5,4},{6,5},{7,6},{8,7},{9,8},{10,9... | collective-permute-start | bytes 2359304 | tf_op jit(solution)/shard_map/ppermute | solution.py:346
  14.5 80.5 %collective-permute-start.1 = (bf16[1,2,3,64,1024]{4,3,2,1,0:T(8,128)(2,1)}, bf16[1,2,3,64,1024]{4,3,2,1,0:T(8,128)(2,1)}, u32[]{:S(2)}, u32[]{:S(2)}) collective-permute-start(bf16[1,2,3,64,1024]{4,3,2,1,0:T(8,128)(2,1)} %get-tuple-element.10), channel_id=1, source_target_pairs={{0,15},{1,0},{2,1},{3,2},{4,3},{5,4},{6,5},{7,6},{8,7},{9,8},{10,9... | collective-permute-start | bytes 2359304 | tf_op jit(solution)/shard_map/ppermute | solution.py:346
  15.2 85.8 %collective-permute-start.2 = (bf16[1,2,3,64,1024]{4,3,2,1,0:T(8,128)(2,1)}, bf16[1,2,3,64,1024]{4,3,2,1,0:T(8,128)(2,1)}, u32[]{:S(2)}, u32[]{:S(2)}) collective-permute-start(bf16[1,2,3,64,1024]{4,3,2,1,0:T(8,128)(2,1)} %get-tuple-element.12), channel_id=1, source_target_pairs={{0,15},{1,0},{2,1},{3,2},{4,3},{5,4},{6,5},{7,6},{8,7},{9,8},{10,9... | collective-permute-start | bytes 2359304 | tf_op jit(solution)/shard_map/ppermute | solution.py:346
  15.2 91.9 %collective-permute-start.3 = (bf16[1,2,3,64,1024]{4,3,2,1,0:T(8,128)(2,1)}, bf16[1,2,3,64,1024]{4,3,2,1,0:T(8,128)(2,1)S(1)}, u32[]{:S(2)}, u32[]{:S(2)}) collective-permute-start(bf16[1,2,3,64,1024]{4,3,2,1,0:T(8,128)(2,1)} %get-tuple-element.11), channel_id=1, source_target_pairs={{0,15},{1,0},{2,1},{3,2},{4,3},{5,4},{6,5},{7,6},{8,7},{9,8},{10,9... | collective-permute-start | bytes 2359304 | tf_op jit(solution)/shard_map/ppermute | solution.py:346
  38.6 50.5 %slice-start = ((s8[6291456]{0:T(1024)(128)(4,1)}), s8[2097152]{0:T(1024)(128)(4,1)S(1)}, s32[]{:S(2)}) async-start(s8[6291456]{0:T(1024)(128)(4,1)} %bitcast.101), calls=%async_computation | async-start | bytes 4194304
  49.8 2.8 %copy-start = (bf16[4,2,3,128,1,1024]{5,3,4,2,1,0:T(8,128)(2,1)S(1)}, bf16[4,2,3,128,1,1024]{5,3,4,2,1,0:T(8,128)(2,1)}, u32[]{:S(2)}) copy-start(bf16[4,2,3,128,1,1024]{5,3,4,2,1,0:T(8,128)(2,1)} %param.5) | copy-start | bytes 18874372
  52.6 36.5 %slice-start.1 = ((s8[6291456]{0:T(1024)(128)(4,1)}), s8[4194304]{0:T(1024)(128)(4,1)S(1)}, s32[]{:S(2)}) async-start(s8[6291456]{0:T(1024)(128)(4,1)} %bitcast.101), calls=%async_computation.1 | async-start | bytes 8388608

commit v2 on v1

v2 whole, which is shorter than its diff:
```python
import functools
import math

import jax
import jax.numpy as jnp
from jax import lax
from jax.experimental import pallas as pl
from jax.experimental.pallas import tpu as pltpu
from jax.sharding import PartitionSpec as P

BLK = 4
LY = 32
LZ = 32
SITES = 256
ROWS = 16
CHUNKS = 2
MESH = pl.DeviceIdType.MESH

epsilon_cycles = ((0, 1, 2), (1, 2, 0), (2, 0, 1))


def phase_row(momentum, x_site, extent, sites):
    site = lax.broadcasted_iota(jnp.int32, (1, sites), 1)
    x_turn = lax.rem(lax.rem(momentum[0] * x_site, extent) + extent, extent)
    y_turns = lax.rem(lax.rem(momentum[1] * (site // LZ), LY) + LY, LY).astype(jnp.float32) / LY
    z_turns = lax.rem(lax.rem(momentum[2] * (site % LZ), LZ) + LZ, LZ).astype(jnp.float32) / LZ
    angles = -2.0 * math.pi * (x_turn.astype(jnp.float32) / extent + y_turns + z_turns)
    return jnp.cos(angles), jnp.sin(angles)


def stage_rows(extent, offset, momentum, vec_ref, link_ref, wide_ref, link_rows, lead_rows, weights):
    nev, sites = vec_ref.shape[3:]
    for row in range(3):
        for column in range(3):
            at = 2 * (3 * row + column)
            link_rows[at : at + 2] = link_ref[0, 0, row, column].astype(jnp.float32)
    cosine, sine = phase_row(momentum, lax.axis_index("space"), extent, sites)
    base = pl.multiple_of(jnp.minimum((offset // 16) * 16, nev - 32), 16)
    for c in range(3):
        for r in range(2):
            wide_ref[r] = vec_ref[0, r, c, pl.ds(base, 32)].astype(jnp.float32)
        for a in range(BLK):
            now_re = wide_ref[0, pl.ds(offset - base + a, 1)]
            now_im = wide_ref[1, pl.ds(offset - base + a, 1)]
            at = 2 * (c * BLK + a)
            lead_rows[at : at + 1] = now_re * cosine - now_im * sine
            lead_rows[at + 1 : at + 2] = now_re * sine + now_im * cosine
    for part in range(sites // SITES):
        for r in range(2):
            for k in range(3):
                weights[part, r * nev : (r + 1) * nev, k * SITES : (k + 1) * SITES] = vec_ref[
                    0, r, k, :, part * SITES : (part + 1) * SITES
                ]


def dot_rows(left, right):
    return lax.dot_general(left, right, (((1,), (1,)), ((), ())), preferred_element_type=jnp.float32)


def sums_of(source_at, count, sites, link_rows, lead_rows, weights, prods, acc_ref):
    share = 2 * BLK * ROWS

    for part in range(sites // SITES):
        lanes = slice(part * SITES, (part + 1) * SITES)
        prod_ref = prods[part % 2]
        last_ref = prods[(part + 1) % 2]

        def rows_step(step, carry, part=part, lanes=lanes, prod_ref=prod_ref, last_ref=last_ref):
            if part > 0:
                rows = pl.ds(pl.multiple_of(step * share, share), share)
                now = dot_rows(last_ref[rows], weights[part - 1])
                acc_ref[rows] = now if part == 1 else acc_ref[rows] + now
            first = pl.multiple_of(step * ROWS, ROWS)
            src_re = [source_at(0, c, first, lanes) for c in range(3)]
            src_im = [source_at(1, c, first, lanes) for c in range(3)]
            part_re = []
            part_im = []
            for row in range(3):
                acc_re = None
                acc_im = None
                for column in range(3):
                    at = 2 * (row * 3 + column)
                    link_re = link_rows[at : at + 1, lanes]
                    link_im = link_rows[at + 1 : at + 2, lanes]
                    now_re = link_re * src_re[column] - link_im * src_im[column]
                    now_im = link_re * src_im[column] + link_im * src_re[column]
                    acc_re = now_re if acc_re is None else acc_re + now_re
                    acc_im = now_im if acc_im is None else acc_im + now_im
                part_re.append(acc_re.astype(jnp.bfloat16).astype(jnp.float32))
                part_im.append(acc_im.astype(jnp.bfloat16).astype(jnp.float32))
            for a in range(BLK):
                lead_re = []
                lead_im = []
                for c in range(3):
                    at = 2 * (c * BLK + a)
                    lead_re.append(lead_rows[at : at + 1, lanes])
                    lead_im.append(lead_rows[at + 1 : at + 2, lanes])
                for one, two, out in epsilon_cycles:
                    prod_re = (
                        lead_re[one] * part_re[two]
                        - lead_im[one] * part_im[two]
                        - lead_re[two] * part_re[one]
                        + lead_im[two] * part_im[one]
                    )
                    prod_im = (
                        lead_re[one] * part_im[two]
                        + lead_im[one] * part_re[two]
                        - lead_re[two] * part_im[one]
                        - lead_im[two] * part_re[one]
                    )
                    where = slice(out * SITES, (out + 1) * SITES)
                    at_re = pl.multiple_of(a * count + first, ROWS)
                    at_im = pl.multiple_of((BLK + a) * count + first, ROWS)
                    prod_ref[pl.ds(at_re, ROWS), where] = prod_re.astype(jnp.bfloat16)
                    prod_ref[pl.ds(at_im, ROWS), where] = prod_im.astype(jnp.bfloat16)
            return carry

        lax.fori_loop(0, count // ROWS, rows_step, 0)


def write_out(acc_ref, last_ref, last_weights, out_ref, count, nev, norm_factor):
    half = BLK * count
    for a in range(BLK):
        at_re = slice(a * count, (a + 1) * count)
        at_im = slice(half + a * count, half + (a + 1) * count)
        rows_re = acc_ref[at_re] + dot_rows(last_ref[at_re], last_weights[...])
        rows_im = acc_ref[at_im] + dot_rows(last_ref[at_im], last_weights[...])
        out_re = (rows_re[:, :nev] - rows_im[:, nev:]) * norm_factor
        out_im = (rows_re[:, nev:] + rows_im[:, :nev]) * norm_factor
        for g in range(count // 8):
            out_ref[g, a] = out_re[g * 8 : g * 8 + 8]
            out_ref[g, BLK + a] = out_im[g * 8 : g * 8 + 8]


def shift_sources(second, vec_ref, src_ref):
    nev, sites = vec_ref.shape[3:]
    lane = lax.broadcasted_iota(jnp.int32, (ROWS, sites), 1)

    def rows_step(i, carry):
        rows = pl.ds(pl.multiple_of(i * ROWS, ROWS), ROWS)
        for r in range(2):
            for c in range(3):
                now = vec_ref[0, r, c, rows].astype(jnp.float32)
                if second:
                    moved = pltpu.roll(now, sites - LZ, 1)
                else:
                    moved = jnp.where(
                        lane % LZ == LZ - 1,
                        pltpu.roll(now, LZ - 1, 1),
                        pltpu.roll(now, sites - 1, 1),
                    )
                src_ref[r, c, rows] = moved
        return carry

    lax.fori_loop(0, nev // ROWS, rows_step, 0)


def sums_kernel(place, extent, norm_factor, order, directions, offsets, momentum, vec_ref, link_ref, *refs):
    nev, sites = vec_ref.shape[3:]
    now = order[place]
    if len(refs) == 9:
        src_ref, out_ref, wide_ref, link_rows, lead_rows, weights, prod_a, prod_b, acc_ref = refs
        count = src_ref.shape[2]

        def source_at(r, c, first, lanes):
            return src_ref[r, c, pl.ds(first, ROWS), lanes].astype(jnp.float32)
    else:
        out_ref, wide_ref, link_rows, lead_rows, weights, prod_a, prod_b, acc_ref, moved_ref, _ = refs
        count = nev

        def source_at(r, c, first, lanes):
            return moved_ref[r, c, pl.ds(first, ROWS), lanes]

        @pl.when(directions[now] == 1)
        def _():
            shift_sources(True, vec_ref, moved_ref)

        @pl.when(directions[now] != 1)
        def _():
            shift_sources(False, vec_ref, moved_ref)

    stage_rows(extent, offsets[now], momentum, vec_ref, link_ref, wide_ref, link_rows, lead_rows, weights)
    sums_of(source_at, count, sites, link_rows, lead_rows, weights, (prod_a, prod_b), acc_ref)
    parts = sites // SITES
    write_out(acc_ref, (prod_a, prod_b)[(parts - 1) % 2], weights.at[parts - 1], out_ref, count, nev, norm_factor)


def slice_sums(scalars, vectors, links, source, place, extent, norm_factor):
    _, _, _, nev, sites = vectors.shape
    parts = sites // SITES
    count = nev if source is None else source.shape[2]
    operands = [vectors, links] + ([] if source is None else [source])
    in_specs = [
        pl.BlockSpec((1, 2, 3, nev, sites), lambda i, order, *_: (order[place], 0, 0, 0, 0)),
        pl.BlockSpec(
            (1, 1, 3, 3, 2, sites),
            lambda i, order, directions, *_: (order[place], directions[order[place]], 0, 0, 0, 0),
        ),
    ]
    scratch = [
        pltpu.VMEM((2, 32, sites), jnp.float32),
        pltpu.VMEM((18, sites), jnp.float32),
        pltpu.VMEM((6 * BLK, sites), jnp.float32),
        pltpu.VMEM((parts, 2 * nev, 3 * SITES), jnp.bfloat16),
        pltpu.VMEM((2 * BLK * count, 3 * SITES), jnp.bfloat16),
        pltpu.VMEM((2 * BLK * count, 3 * SITES), jnp.bfloat16),
        pltpu.VMEM((2 * BLK * count, 2 * nev), jnp.float32),
    ]
    if source is None:
        scratch += [pltpu.VMEM((2, 3, nev, sites), jnp.float32), pltpu.VMEM((8, 128), jnp.float32)]
    else:
        in_specs.append(pl.BlockSpec((2, 3, count, sites), lambda i, *_: (0, 0, 0, 0)))
    return pl.pallas_call(
        functools.partial(sums_kernel, place, extent, norm_factor),
        out_shape=jax.ShapeDtypeStruct((count // 8, 2 * BLK, 8, nev), jnp.float32),
        grid_spec=pltpu.PrefetchScalarGridSpec(
            num_scalar_prefetch=4,
            grid=(1,),
            in_specs=in_specs,
            out_specs=pl.BlockSpec((count // 8, 2 * BLK, 8, nev), lambda i, *_: (0, 0, 0, 0)),
            scratch_shapes=scratch,
        ),
        compiler_params=pltpu.CompilerParams(vmem_limit_bytes=40 * 2**20),
        cost_estimate=pl.CostEstimate(
            flops=100 * 2 * BLK * count * 3 * sites, bytes_accessed=2 * 2**20, transcendentals=0
        ),
        name="inner_sums" if source is None else "outer_sums",
    )(*scalars, *operands)


def scatter_kernel(groups, part_ref, out_ref, send_one, send_two, send_three, recv_one, recv_two, recv_three, sum_one, sum_two, sems_out, sems_in):
    me = lax.axis_index("space")
    core = me % 2
    row = (me // 2) % 2
    group = me // 4
    pair = me + 1 - 2 * core
    across = me + 2 - 4 * row
    others = [(group + step) % groups for step in range(1, groups)]
    barrier = pltpu.get_barrier_semaphore()
    for partner in [pair, across] + [other * 4 + row * 2 + core for other in others]:
        pl.semaphore_signal(barrier, inc=1, device_id={"space": partner}, device_id_type=MESH)
    pl.semaphore_wait(barrier, groups + 1)

    def copy(source, target, number, partner):
        return pltpu.make_async_remote_copy(
            src_ref=source, dst_ref=target, send_sem=sems_out.at[number], recv_sem=sems_in.at[number],
            device_id={"space": partner}, device_id_type=MESH,
        )

    for z in range(groups):
        for y in range(2):
            send_one[z, y] = part_ref[z, y, 1 - core].astype(jnp.bfloat16)
    first = copy(send_one, recv_one, 0, pair)
    first.start()
    first.wait()
    for z in range(groups):
        got = part_ref[z, 1 - row, core] + recv_one[z, 1 - row].astype(jnp.float32)
        send_two[z] = got.astype(jnp.bfloat16)
    second = copy(send_two, recv_two, 1, across)
    second.start()
    for z in range(groups):
        sum_one[z] = part_ref[z, row, core] + recv_one[z, row].astype(jnp.float32)
    second.wait()
    for z in range(groups):
        sum_two[z] = sum_one[z] + recv_two[z].astype(jnp.float32)
        send_three[z] = sum_two[z].astype(jnp.bfloat16)
    copies = []
    for step, other in enumerate(others):
        copies.append(copy(send_three.at[other], recv_three.at[step], 2 + step, other * 4 + row * 2 + core))
        copies[-1].start()
    total = sum_two[group]
    for step in range(groups - 1):
        copies[step].wait()
        total = total + recv_three[step].astype(jnp.float32)
    out_ref[...] = total


def scatter_sum(part, number):
    devices, rows, columns = part.shape
    groups = devices // 4
    whole = pl.BlockSpec(memory_space=pltpu.VMEM)
    bf16 = jnp.bfloat16
    return pl.pallas_call(
        functools.partial(scatter_kernel, groups),
        out_shape=jax.ShapeDtypeStruct((rows, columns), jnp.float32),
        in_specs=[whole],
        out_specs=whole,
        scratch_shapes=[
            pltpu.VMEM((groups, 2, rows, columns), bf16),
            pltpu.VMEM((groups, rows, columns), bf16),
            pltpu.VMEM((groups, rows, columns), bf16),
            pltpu.VMEM((groups, 2, rows, columns), bf16),
            pltpu.VMEM((groups, rows, columns), bf16),
            pltpu.VMEM((groups, rows, columns), bf16),
            pltpu.VMEM((groups, rows, columns), jnp.float32),
            pltpu.VMEM((groups, rows, columns), jnp.float32),
            pltpu.SemaphoreType.DMA((groups + 1,)),
            pltpu.SemaphoreType.DMA((groups + 1,)),
        ],
        compiler_params=pltpu.CompilerParams(
            collective_id=number, has_side_effects=True, vmem_limit_bytes=40 * 2**20
        ),
        name="scatter_sum",
    )(part.reshape(groups, 2, 2, rows, columns))


def by_owner(part, devices):
    slices, tiles, parts, eight, nev = part.shape
    own = tiles * eight // devices
    if own == eight:
        moved = jnp.transpose(part, (1, 0, 2, 3, 4))
    else:
        flat = jnp.transpose(part, (0, 2, 1, 3, 4)).reshape(slices, parts, devices, own, nev)
        moved = jnp.transpose(flat, (2, 0, 1, 3, 4))
    return moved.reshape(devices, slices * parts * own, nev)


def on_device(eigenvectors, link_field, momentum, directions, offsets):
    devices = lax.axis_size("space")
    slices, _, _, nev, planes, sites = eigenvectors.shape
    extent_x = planes * devices
    norm_factor = 1.0 / math.sqrt(extent_x * LY * LZ)
    vectors = eigenvectors.reshape(slices, 2, 3, nev, sites)

    inner = (directions != 0).astype(jnp.int32)
    numbers = jnp.arange(slices, dtype=jnp.int32)
    before = (inner[None] < inner[:, None]) | (
        (inner[None] == inner[:, None]) & (numbers[None] < numbers[:, None])
    )
    rank = jnp.sum(before.astype(jnp.int32), axis=1)
    order = [jnp.sum(jnp.where(rank == place, numbers, 0)) for place in range(slices)]
    half = slices // 2

    size = nev // CHUNKS
    pairs = [(source, (source - 1) % devices) for source in range(devices)]
    above = []
    for place in range(half):
        for chunk in range(CHUNKS):
            piece = lax.dynamic_slice(
                vectors, (order[place], 0, 0, chunk * size, 0), (1, 2, 3, size, sites)
            )
            above.append(lax.ppermute(piece, "space", pairs)[0])

    links = jnp.transpose(
        link_field.reshape(slices, 3, 2, 3, 3, sites), (0, 1, 3, 4, 2, 5)
    )
    scalars = (jnp.stack(order), directions, offsets, momentum)
    sums_at = functools.partial(slice_sums, scalars, vectors, links, extent=extent_x, norm_factor=norm_factor)
    results = [None] * slices
    for place in range(half, slices):
        part = by_owner(sums_at(None, place)[None], devices)
        results[place] = lax.psum_scatter(part, "space", scatter_dimension=0, tiled=True)
    for place in range(half):
        pieces = [sums_at(above[place * CHUNKS + chunk], place) for chunk in range(CHUNKS)]
        part = by_owner(jnp.concatenate(pieces)[None], devices)
        if place < half - 1:
            results[place] = lax.psum_scatter(part, "space", scatter_dimension=0, tiled=True)
        else:
            results[place] = scatter_sum(part, 0)[None]

    own = nev // devices
    both = jnp.concatenate(results).reshape(slices, 2, BLK, own, nev)
    return jnp.take(both, rank, axis=0, mode="clip")


def solution(mesh):
    placed = (
        P("cfg", None, None, None, "space", None),
        P("cfg", None, None, None, None, "space", None),
        P(),
        P(),
        P(),
    )
    return jax.shard_map(
        on_device,
        mesh=mesh,
        in_specs=placed,
        out_specs=P("cfg", None, None, "space", None),
        check_vma=False,
    )
```

time: 127 us -> 224 us (1.76)
  waiting for transfers between devices: 0.01 us -> 115 us
  Pallas kernels: 71.5 us -> 61.5 us
  between operations: 23.5 us -> 17 us
  other arithmetic: 9.64 us -> 5.81 us
    reduce_scatter x0 -> x3, waiting for transfers between devices: none -> 115 us  [on_device(): lax.psum_scatter(part, 'space', scatter_dimension=0, tiled=True)]
    pallas_call x2 -> x1, Pallas kernels: 24.7 us -> 10.4 us  [scatter_sum(): pl.pallas_call(functools.partial(scatter_kernel, groups), out_shape=jax.S...]
    unnamed x15 -> x24, local copies, waits for them, and re-layouts: 3.72 us -> 11.4 us
    pallas_call x5 -> x6, Pallas kernels: 46.8 us -> 51 us  [slice_sums(): pl.pallas_call(functools.partial(sums_kernel, place, extent, norm_factor)...]
    dynamic_slice x6 -> x0, local copies, waits for them, and re-layouts: 3.87 us -> none  [the longest x5 3.19 us: on_device(): lax.dynamic_slice(link_field, (now, directions[now], 0, 0, 0, 0, 0), (1,...]
  transfers between devices with their start and end apart: 4 -> 7, of which waited for: 0 -> 2; matrix products, arithmetic and copies ran while one was open for 12% -> 2% of each run, Pallas kernels for 43% -> 22%
where the time goes in v2:
time: 224 us; the launch traced here: 223 us
  waiting for transfers between devices  115 us (51%)
  Pallas kernels  61.5 us (27%)
  between operations  17 us (8%)
  local copies, waits for them, and re-layouts  16.4 us (7%)
  starting transfers between devices  7.32 us (3%)
  other arithmetic  5.81 us (3%)
    reduce_scatter x3, waiting for transfers between devices, on_device(): lax.psum_scatter(part, 'space', scatter_dimension=0, tiled=True)  115 us
    pallas_call x6, Pallas kernels, slice_sums(): pl.pallas_call(functools.partial(sums_kernel, place, extent, norm_factor)...  51 us
    unnamed x24, local copies, waits for them, and re-layouts  11.4 us
    pallas_call x1, Pallas kernels, scatter_sum(): pl.pallas_call(functools.partial(scatter_kernel, groups), out_shape=jax.S...  10.4 us
    ppermute x4, starting transfers between devices, on_device(): above.append(lax.ppermute(piece, 'space', pairs)[0])  7.24 us
  transfers between devices with their start and end apart: 7, of which 2 were waited for; matrix products, arithmetic and copies ran while one was open for 2% of the time, Pallas kernels for 22%

profile of v2, /device:TPU:0, one launch (start us, length us, event | category | flops | bytes accessed | tf_op | source)
XLA Modules:
  0.0 223.3 jit_solution(18292117348277853783)
XLA Ops:
  6.5 0.7 compare_convert_fusion
  7.2 0.2 convert_reduce_fusion
  7.4 0.7 fusion.2
  8.1 2.6 %pad_add_fusion.order = s32[4]{0:T(128)S(1)} fusion(s32[1]{0:T(128)} %bitcast.3, s32[1]{0:T(128)} %bitcast.2, s32[1]{0:T(128)} %bitcast.1, s32[1]{0:T(128)} %bitcast), kind=kLoop, calls=%fused_computation.22 | loop fusion | flops 12 | bytes 32 | tf_op jit(solution)/shard_map/stack | solution.py:347
  10.7 2.8 %copy-done = bf16[4,2,3,128,1,1024]{5,3,4,2,1,0:T(8,128)(2,1)S(1)} copy-done((bf16[4,2,3,128,1,1024]{5,3,4,2,1,0:T(8,128)(2,1)S(1)}, bf16[4,2,3,128,1,1024]{5,3,4,2,1,0:T(8,128)(2,1)}, u32[]{:S(2)}) %copy-start) | copy-done | bytes 6291480
  13.4 1.0 copy-done.4
  14.5 0.7 copy-done.6
  15.1 0.7 copy-done.8
  15.8 0.7 copy-done.10
  16.4 12.3 %inner_sums.2 = f32[16,8,8,128]{3,2,1,0:T(8,128)} custom-call(s32[4]{0:T(128)S(1)} %pad_add_fusion.order, s32[4]{0:T(128)S(1)} %copy-done.6, s32[4]{0:T(128)S(1)} %copy-done.8, s32[3]{0:T(128)S(1)} %copy-done.10, bf16[4,2,3,128,1024]{4,3,2,1,0:T(8,128)(2,1)S(1)} %bitcast.29, bf16[4,3,3,3,2,1024]{5,4,3,2,1,0:T(2,128)(2,1)S(1)} %bitcast.35), custom_call_target="tpu_custom_call" | custom-call | flops 314572800 | bytes 2097152 | tf_op jit(solution)/shard_map/inner_sums/pallas_call | solution.py:213
  28.8 0.0 reduce-scatter.6.cloned.1.call-update
  28.8 0.0 reduce-scatter.8.cloned.1.call-start
  32.7 3.8 %dynamic-slice_bitcast_fusion.3 = (bf16[1,2,3,64,1024]{4,3,2,1,0:T(8,128)(2,1)}, bf16[1,2,3,64,1024]{4,3,2,1,0:T(8,128)(2,1)}, bf16[1,2,3,64,1024]{4,3,2,1,0:T(8,128)(2,1)}, bf16[1,2,3,64,1024]{4,3,2,1,0:T(8,128)(2,1)}) fusion(bf16[4,2,3,128,1,1024]{5,3,4,2,1,0:T(8,128)(2,1)} %param.5, s32[]{:T(128)S(6)} %select_n.25, s32[]{:T(128)S(6)} %select_n.26), kind=kLoop, calls=%fused_computation.4 | loop fusion | bytes 6291464 | tf_op jit(solution)/shard_map/dynamic_slice | solution.py:339
  36.5 5.4 %collective-permute-start = (bf16[1,2,3,64,1024]{4,3,2,1,0:T(8,128)(2,1)}, bf16[1,2,3,64,1024]{4,3,2,1,0:T(8,128)(2,1)}, u32[]{:S(2)}, u32[]{:S(2)}) collective-permute-start(bf16[1,2,3,64,1024]{4,3,2,1,0:T(8,128)(2,1)} %get-tuple-element.9), channel_id=1, source_target_pairs={{0,15},{1,0},{2,1},{3,2},{4,3},{5,4},{6,5},{7,6},{8,7},{9,8},{10,9... | collective-permute-start | bytes 2359304 | tf_op jit(solution)/shard_map/ppermute | solution.py:342
  41.9 0.7 collective-permute-start.1
  42.6 12.7 %inner_sums.3 = f32[16,8,8,128]{3,2,1,0:T(8,128)} custom-call(s32[4]{0:T(128)S(1)} %pad_add_fusion.order, s32[4]{0:T(128)S(1)} %copy-done.7, s32[4]{0:T(128)S(1)} %copy-done.9, s32[3]{0:T(128)S(1)} %copy-done.10, bf16[4,2,3,128,1024]{4,3,2,1,0:T(8,128)(2,1)S(1)} %bitcast.30, bf16[4,3,3,3,2,1024]{5,4,3,2,1,0:T(2,128)(2,1)S(1)} %bitcast.36), custom_call_target="tpu_custom_call" | custom-call | flops 314572800 | bytes 2097152 | tf_op jit(solution)/shard_map/inner_sums/pallas_call | solution.py:213
  55.4 0.0 reduce-scatter.4.cloned.1.call-start
  55.4 0.4 collective-permute-start.2
  55.9 0.7 collective-permute-start.3
  56.6 2.8 %copy-done.2 = bf16[4,2,3,128,1,1024]{5,3,4,2,1,0:T(8,128)(2,1)S(1)} copy-done((bf16[4,2,3,128,1,1024]{5,3,4,2,1,0:T(8,128)(2,1)S(1)}, bf16[4,2,3,128,1,1024]{5,3,4,2,1,0:T(8,128)(2,1)}, u32[]{:S(2)}) %copy-start.2) | copy-done | bytes 6291480
  59.4 7.4 %outer_sums.4 = f32[8,8,8,128]{3,2,1,0:T(8,128)S(1)} custom-call(s32[4]{0:T(128)S(1)} %pad_add_fusion.order, s32[4]{0:T(128)S(1)} %copy-done.7, s32[4]{0:T(128)S(1)} %copy-done.9, s32[3]{0:T(128)S(1)} %copy-done.11, bf16[4,2,3,128,1024]{4,3,2,1,0:T(8,128)(2,1)S(1)} %bitcast.31, bf16[4,3,3,3,2,1024]{5,4,3,2,1,0:T(2,128)(2,1)S(1)} %bitcast.37, ...), custom_call_target="tpu_custom_call" | custom-call | flops 157286400 | bytes 2097152 | tf_op jit(solution)/shard_map/outer_sums/pallas_call | solution.py:213
  66.7 6.2 %outer_sums.5 = f32[8,8,8,128]{3,2,1,0:T(8,128)S(1)} custom-call(s32[4]{0:T(128)S(1)} %pad_add_fusion.order, s32[4]{0:T(128)S(1)} %copy-done.7, s32[4]{0:T(128)S(1)} %copy-done.9, s32[3]{0:T(128)S(1)} %copy-done.11, bf16[4,2,3,128,1024]{4,3,2,1,0:T(8,128)(2,1)S(1)} %bitcast.32, bf16[4,3,3,3,2,1024]{5,4,3,2,1,0:T(2,128)(2,1)S(1)} %bitcast.38, ...), custom_call_target="tpu_custom_call" | custom-call | flops 157286400 | bytes 2097152 | tf_op jit(solution)/shard_map/outer_sums/pallas_call | solution.py:213
  72.9 0.8 maximum_bitcast_fusion
  73.8 2.8 %copy-done.3 = bf16[4,2,3,128,1,1024]{5,3,4,2,1,0:T(8,128)(2,1)S(1)} copy-done((bf16[4,2,3,128,1,1024]{5,3,4,2,1,0:T(8,128)(2,1)S(1)}, bf16[4,2,3,128,1,1024]{5,3,4,2,1,0:T(8,128)(2,1)}, u32[]{:S(2)}) %copy-start.3) | copy-done | bytes 6291480
  76.6 6.2 %outer_sums.6 = f32[8,8,8,128]{3,2,1,0:T(8,128)S(1)} custom-call(s32[4]{0:T(128)S(1)} %pad_add_fusion.order, s32[4]{0:T(128)S(1)} %copy-done.7, s32[4]{0:T(128)S(1)} %copy-done.9, s32[3]{0:T(128)S(1)} %copy-done.11, bf16[4,2,3,128,1024]{4,3,2,1,0:T(8,128)(2,1)S(1)} %bitcast.33, bf16[4,3,3,3,2,1024]{5,4,3,2,1,0:T(2,128)(2,1)S(1)} %bitcast.39, ...), custom_call_target="tpu_custom_call" | custom-call | flops 157286400 | bytes 2097152 | tf_op jit(solution)/shard_map/outer_sums/pallas_call | solution.py:213
  82.8 6.2 %outer_sums.7 = f32[8,8,8,128]{3,2,1,0:T(8,128)S(1)} custom-call(s32[4]{0:T(128)S(1)} %pad_add_fusion.order, s32[4]{0:T(128)S(1)} %copy-done.7, s32[4]{0:T(128)S(1)} %copy-done.9, s32[3]{0:T(128)S(1)} %copy-done.11, bf16[4,2,3,128,1024]{4,3,2,1,0:T(8,128)(2,1)S(1)} %bitcast.34, bf16[4,3,3,3,2,1024]{5,4,3,2,1,0:T(2,128)(2,1)S(1)} %bitcast.40, ...), custom_call_target="tpu_custom_call" | custom-call | flops 157286400 | bytes 2097152 | tf_op jit(solution)/shard_map/outer_sums/pallas_call | solution.py:213
  89.1 10.4 %scatter_sum.1 = f32[64,128]{1,0:T(8,128)S(1)} custom-call(f32[4,2,2,64,128]{4,3,2,1,0:T(8,128)S(1)} %bitcast.41), custom_call_target="tpu_custom_call" | custom-call | tf_op jit(solution)/shard_map/scatter_sum/pallas_call | solution.py:283
  99.5 0.0 reduce-scatter.6.cloned.1.call-done
  99.5 56.8 %reduce-scatter.8.cloned.1.call-done = f32[1,64,128]{2,1,0:T(8,128)} async-done(((f32[16,64,128]{2,1,0:T(8,128)}), f32[1,64,128]{2,1,0:T(8,128)}) %reduce-scatter.8.cloned.1.call-update) | async-done | bytes 32784 | tf_op jit(solution)/shard_map/reduce_scatter | solution.py:352
  156.3 58.4 %reduce-scatter.4.cloned.1.call-done = f32[1,64,128]{2,1,0:T(8,128)} async-done(((f32[16,64,128]{2,1,0:T(8,128)}), f32[1,64,128]{2,1,0:T(8,128)}) %reduce-scatter.4.cloned.1.call-update) | async-done | bytes 32784 | tf_op jit(solution)/shard_map/reduce_scatter | solution.py:357
  214.7 0.8 pad_maximum_fusion.1
  215.5 1.2 gather_fusion
  (26 shorter events, 0.1 us)
Async XLA Ops:
  6.5 93.0 %reduce-scatter.6.cloned.1.call-start = ((), (), s32[]{:S(2)}) async-start(), calls=%async_computation.4 | async-start | bytes 557056 | tf_op jit(solution)/shard_map/reduce_scatter | solution.py:352
  10.7 2.8 %copy-start = (bf16[4,2,3,128,1,1024]{5,3,4,2,1,0:T(8,128)(2,1)S(1)}, bf16[4,2,3,128,1,1024]{5,3,4,2,1,0:T(8,128)(2,1)}, u32[]{:S(2)}) copy-start(bf16[4,2,3,128,1,1024]{5,3,4,2,1,0:T(8,128)(2,1)} %param.5) | copy-start | bytes 18874372
  13.4 1.0 copy-start.4
  14.5 0.7 copy-start.6
  15.1 0.7 copy-start.8
  15.8 0.7 copy-start.10
  16.4 26.2 %copy-start.5 = (bf16[4,3,2,3,3,1,1024]{6,2,5,4,3,1,0:T(2,128)(2,1)S(1)}, bf16[4,3,2,3,3,1,1024]{6,2,5,4,3,1,0:T(2,128)(2,1)}, u32[]{:S(2)}) copy-start(bf16[4,3,2,3,3,1,1024]{6,2,5,4,3,1,0:T(2,128)(2,1)} %param.6) | copy-start | bytes 1327108
  16.4 26.2 %copy-start.7 = (s32[4]{0:T(128)S(1)}, s32[4]{0:T(128)}, u32[]{:S(2)}) copy-start(s32[4]{0:T(128)} %directions.11) | copy-start | bytes 52
  16.4 26.2 %copy-start.9 = (s32[4]{0:T(128)S(1)}, s32[4]{0:T(128)}, u32[]{:S(2)}) copy-start(s32[4]{0:T(128)} %offsets.11) | copy-start | bytes 52
  28.8 127.6 %reduce-scatter.8.cloned.1.call-start = ((), (), s32[]{:S(2)}) async-start(), calls=%async_computation.5 | async-start | bytes 557056 | tf_op jit(solution)/shard_map/reduce_scatter | solution.py:352
  32.7 10.0 %copy-start.1 = (bf16[4,2,3,128,1,1024]{5,3,4,2,1,0:T(8,128)(2,1)S(1)}, bf16[4,2,3,128,1,1024]{5,3,4,2,1,0:T(8,128)(2,1)}, u32[]{:S(2)}) copy-start(bf16[4,2,3,128,1,1024]{5,3,4,2,1,0:T(8,128)(2,1)} %param.5) | copy-start | bytes 18874372
  32.7 23.9 %copy-start.11 = (s32[3]{0:T(128)S(1)}, s32[3]{0:T(128)}, u32[]{:S(2)}) copy-start(s32[3]{0:T(128)} %momentum.11) | copy-start | bytes 40
  36.5 20.1 %collective-permute-start = (bf16[1,2,3,64,1024]{4,3,2,1,0:T(8,128)(2,1)}, bf16[1,2,3,64,1024]{4,3,2,1,0:T(8,128)(2,1)}, u32[]{:S(2)}, u32[]{:S(2)}) collective-permute-start(bf16[1,2,3,64,1024]{4,3,2,1,0:T(8,128)(2,1)} %get-tuple-element.9), channel_id=1, source_target_pairs={{0,15},{1,0},{2,1},{3,2},{4,3},{5,4},{6,5},{7,6},{8,7},{9,8},{10,9... | collective-permute-start | bytes 2359304 | tf_op jit(solution)/shard_map/ppermute | solution.py:342
  41.9 24.8 %collective-permute-start.1 = (bf16[1,2,3,64,1024]{4,3,2,1,0:T(8,128)(2,1)}, bf16[1,2,3,64,1024]{4,3,2,1,0:T(8,128)(2,1)S(1)}, u32[]{:S(2)}, u32[]{:S(2)}) collective-permute-start(bf16[1,2,3,64,1024]{4,3,2,1,0:T(8,128)(2,1)} %get-tuple-element.10), channel_id=1, source_target_pairs={{0,15},{1,0},{2,1},{3,2},{4,3},{5,4},{6,5},{7,6},{8,7},{9,8},{10,9... | collective-permute-start | bytes 2359304 | tf_op jit(solution)/shard_map/ppermute | solution.py:342
  55.4 159.3 %reduce-scatter.4.cloned.1.call-start = ((), (), s32[]{:S(2)}) async-start(), calls=%async_computation.3 | async-start | bytes 557056 | tf_op jit(solution)/shard_map/reduce_scatter | solution.py:357
  55.4 18.4 %collective-permute-start.2 = (bf16[1,2,3,64,1024]{4,3,2,1,0:T(8,128)(2,1)}, bf16[1,2,3,64,1024]{4,3,2,1,0:T(8,128)(2,1)S(1)}, u32[]{:S(2)}, u32[]{:S(2)}) collective-permute-start(bf16[1,2,3,64,1024]{4,3,2,1,0:T(8,128)(2,1)} %get-tuple-element.12), channel_id=1, source_target_pairs={{0,15},{1,0},{2,1},{3,2},{4,3},{5,4},{6,5},{7,6},{8,7},{9,8},{10,9... | collective-permute-start | bytes 2359304 | tf_op jit(solution)/shard_map/ppermute | solution.py:342
  55.9 26.9 %collective-permute-start.3 = (bf16[1,2,3,64,1024]{4,3,2,1,0:T(8,128)(2,1)}, bf16[1,2,3,64,1024]{4,3,2,1,0:T(8,128)(2,1)S(1)}, u32[]{:S(2)}, u32[]{:S(2)}) collective-permute-start(bf16[1,2,3,64,1024]{4,3,2,1,0:T(8,128)(2,1)} %get-tuple-element.11), channel_id=1, source_target_pairs={{0,15},{1,0},{2,1},{3,2},{4,3},{5,4},{6,5},{7,6},{8,7},{9,8},{10,9... | collective-permute-start | bytes 2359304 | tf_op jit(solution)/shard_map/ppermute | solution.py:342
  56.6 2.8 %copy-start.2 = (bf16[4,2,3,128,1,1024]{5,3,4,2,1,0:T(8,128)(2,1)S(1)}, bf16[4,2,3,128,1,1024]{5,3,4,2,1,0:T(8,128)(2,1)}, u32[]{:S(2)}) copy-start(bf16[4,2,3,128,1,1024]{5,3,4,2,1,0:T(8,128)(2,1)} %param.5) | copy-start | bytes 18874372
  73.8 2.8 %copy-start.3 = (bf16[4,2,3,128,1,1024]{5,3,4,2,1,0:T(8,128)(2,1)S(1)}, bf16[4,2,3,128,1,1024]{5,3,4,2,1,0:T(8,128)(2,1)}, u32[]{:S(2)}) copy-start(bf16[4,2,3,128,1,1024]{5,3,4,2,1,0:T(8,128)(2,1)} %param.5) | copy-start | bytes 18874372
Sparse Core Ops, SparseCore 0:
  28.9 68.5 reduce-scatter.5
  101.5 54.7 reduce-scatter.7
  159.9 54.7 reduce-scatter.3

commit v3 on v2

--- a/solution.py
+++ b/solution.py
@@ -13,7 +13,6 @@
 LZ = 32
 SITES = 256
 ROWS = 16
-CHUNKS = 2
 MESH = pl.DeviceIdType.MESH
 
 epsilon_cycles = ((0, 1, 2), (1, 2, 0), (2, 0, 1))
@@ -32,8 +31,11 @@
     nev, sites = vec_ref.shape[3:]
     for row in range(3):
         for column in range(3):
-            at = 2 * (3 * row + column)
-            link_rows[at : at + 2] = link_ref[0, 0, row, column].astype(jnp.float32)
+            at = 3 * (3 * row + column)
+            pair = link_ref[0, 0, row, column].astype(jnp.float32)
+            link_rows[at : at + 1] = pair[0:1]
+            link_rows[at + 1 : at + 2] = pair[0:1] + pair[1:2]
+            link_rows[at + 2 : at + 3] = pair[1:2] - pair[0:1]
     cosine, sine = phase_row(momentum, lax.axis_index("space"), extent, sites)
     base = pl.multiple_of(jnp.minimum((offset // 16) * 16, nev - 32), 16)
     for c in range(3):
@@ -42,15 +44,22 @@
         for a in range(BLK):
             now_re = wide_ref[0, pl.ds(offset - base + a, 1)]
             now_im = wide_ref[1, pl.ds(offset - base + a, 1)]
-            at = 2 * (c * BLK + a)
-            lead_rows[at : at + 1] = now_re * cosine - now_im * sine
-            lead_rows[at + 1 : at + 2] = now_re * sine + now_im * cosine
+            at = 3 * (c * BLK + a)
+            turned_re = now_re * cosine - now_im * sine
+            turned_im = now_re * sine + now_im * cosine
+            lead_rows[at : at + 1] = turned_re
+            lead_rows[at + 1 : at + 2] = turned_re + turned_im
+            lead_rows[at + 2 : at + 3] = turned_im - turned_re
     for part in range(sites // SITES):
         for r in range(2):
             for k in range(3):
                 weights[part, r * nev : (r + 1) * nev, k * SITES : (k + 1) * SITES] = vec_ref[
                     0, r, k, :, part * SITES : (part + 1) * SITES
                 ]
+
+
+def sum_of(terms):
+    return functools.reduce(lambda left, right: left + right, terms)
 
 
 def dot_rows(left, right):
@@ -73,41 +82,29 @@
             first = pl.multiple_of(step * ROWS, ROWS)
             src_re = [source_at(0, c, first, lanes) for c in range(3)]
             src_im = [source_at(1, c, first, lanes) for c in range(3)]
+            src_sum = [src_re[c] + src_im[c] for c in range(3)]
             part_re = []
             part_im = []
             for row in range(3):
-                acc_re = None
-                acc_im = None
-                for column in range(3):
-                    at = 2 * (row * 3 + column)
-                    link_re = link_rows[at : at + 1, lanes]
-                    link_im = link_rows[at + 1 : at + 2, lanes]
-                    now_re = link_re * src_re[column] - link_im * src_im[column]
-                    now_im = link_re * src_im[column] + link_im * src_re[column]
-                    acc_re = now_re if acc_re is None else acc_re + now_re
-                    acc_im = now_im if acc_im is None else acc_im + now_im
-                part_re.append(acc_re.astype(jnp.bfloat16).astype(jnp.float32))
-                part_im.append(acc_im.astype(jnp.bfloat16).astype(jnp.float32))
+                rows_now = [
+                    [link_rows[at + n : at + n + 1, lanes] for n in range(3)]
+                    for at in (9 * row, 9 * row + 3, 9 * row + 6)
+                ]
+                common = sum_of(rows_now[c][0] * src_sum[c] for c in range(3))
+                minus = sum_of(rows_now[c][1] * src_im[c] for c in range(3))
+                plus = sum_of(rows_now[c][2] * src_re[c] for c in range(3))
+                part_re.append((common - minus).astype(jnp.bfloat16).astype(jnp.float32))
+                part_im.append((common + plus).astype(jnp.bfloat16).astype(jnp.float32))
+            part_sum = [part_re[c] + part_im[c] for c in range(3)]
             for a in range(BLK):
-                lead_re = []
-                lead_im = []
+                lead = []
                 for c in range(3):
-                    at = 2 * (c * BLK + a)
-                    lead_re.append(lead_rows[at : at + 1, lanes])
-                    lead_im.append(lead_rows[at + 1 : at + 2, lanes])
+                    at = 3 * (c * BLK + a)
+                    lead.append([lead_rows[at + n : at + n + 1, lanes] for n in range(3)])
                 for one, two, out in epsilon_cycles:
-                    prod_re = (
-                        lead_re[one] * part_re[two]
-                        - lead_im[one] * part_im[two]
-                        - lead_re[two] * part_re[one]
-                        + lead_im[two] * part_im[one]
-                    )
-                    prod_im = (
-                        lead_re[one] * part_im[two]
-                        + lead_im[one] * part_re[two]
-                        - lead_re[two] * part_im[one]
-                        - lead_im[two] * part_re[one]
-                    )
+                    common = lead[one][0] * part_sum[two] - lead[two][0] * part_sum[one]
+                    prod_re = common - (lead[one][1] * part_im[two] - lead[two][1] * part_im[one])
+                    prod_im = common + (lead[one][2] * part_re[two] - lead[two][2] * part_re[one])
                     where = slice(out * SITES, (out + 1) * SITES)
                     at_re = pl.multiple_of(a * count + first, ROWS)
                     at_im = pl.multiple_of((BLK + a) * count + first, ROWS)
@@ -160,10 +157,10 @@
     now = order[place]
     if len(refs) == 9:
         src_ref, out_ref, wide_ref, link_rows, lead_rows, weights, prod_a, prod_b, acc_ref = refs
-        count = src_ref.shape[2]
+        count = src_ref.shape[3]
 
         def source_at(r, c, first, lanes):
-            return src_ref[r, c, pl.ds(first, ROWS), lanes].astype(jnp.float32)
+            return src_ref[0, r, c, pl.ds(first, ROWS), lanes].astype(jnp.float32)
     else:
         out_ref, wide_ref, link_rows, lead_rows, weights, prod_a, prod_b, acc_ref, moved_ref, _ = refs
         count = nev
@@ -188,7 +185,7 @@
 def slice_sums(scalars, vectors, links, source, place, extent, norm_factor):
     _, _, _, nev, sites = vectors.shape
     parts = sites // SITES
-    count = nev if source is None else source.shape[2]
+    count = nev if source is None else source.shape[3]
     operands = [vectors, links] + ([] if source is None else [source])
     in_specs = [
         pl.BlockSpec((1, 2, 3, nev, sites), lambda i, order, *_: (order[place], 0, 0, 0, 0)),
@@ -199,8 +196,8 @@
     ]
     scratch = [
         pltpu.VMEM((2, 32, sites), jnp.float32),
-        pltpu.VMEM((18, sites), jnp.float32),
-        pltpu.VMEM((6 * BLK, sites), jnp.float32),
+        pltpu.VMEM((27, sites), jnp.float32),
+        pltpu.VMEM((9 * BLK, sites), jnp.float32),
         pltpu.VMEM((parts, 2 * nev, 3 * SITES), jnp.bfloat16),
         pltpu.VMEM((2 * BLK * count, 3 * SITES), jnp.bfloat16),
         pltpu.VMEM((2 * BLK * count, 3 * SITES), jnp.bfloat16),
@@ -209,7 +206,7 @@
     if source is None:
         scratch += [pltpu.VMEM((2, 3, nev, sites), jnp.float32), pltpu.VMEM((8, 128), jnp.float32)]
     else:
-        in_specs.append(pl.BlockSpec((2, 3, count, sites), lambda i, *_: (0, 0, 0, 0)))
+        in_specs.append(pl.BlockSpec((1, 2, 3, count, sites), lambda i, *_: (0, 0, 0, 0, 0)))
     return pl.pallas_call(
         functools.partial(sums_kernel, place, extent, norm_factor),
         out_shape=jax.ShapeDtypeStruct((count // 8, 2 * BLK, 8, nev), jnp.float32),
@@ -228,7 +225,9 @@
     )(*scalars, *operands)
 
 
-def scatter_kernel(groups, part_ref, out_ref, send_one, send_two, send_three, recv_one, recv_two, recv_three, sum_one, sum_two, sems_out, sems_in):
+def scatter_kernel(groups, count, *refs):
+    parts, out_ref = refs[:count], refs[count]
+    send_one, send_two, send_three, recv_one, recv_two, recv_three, sum_one, sems_out, sems_in = refs[count + 1 :]
     me = lax.axis_index("space")
     core = me % 2
     row = (me // 2) % 2
@@ -236,72 +235,77 @@
     pair = me + 1 - 2 * core
     across = me + 2 - 4 * row
     others = [(group + step) % groups for step in range(1, groups)]
+    partners = [other * 4 + row * 2 + core for other in others]
     barrier = pltpu.get_barrier_semaphore()
-    for partner in [pair, across] + [other * 4 + row * 2 + core for other in others]:
+    for partner in [pair, across] + partners:
         pl.semaphore_signal(barrier, inc=1, device_id={"space": partner}, device_id_type=MESH)
     pl.semaphore_wait(barrier, groups + 1)
 
-    def copy(source, target, number, partner):
-        return pltpu.make_async_remote_copy(
+    def start(source, target, number, partner):
+        copy = pltpu.make_async_remote_copy(
             src_ref=source, dst_ref=target, send_sem=sems_out.at[number], recv_sem=sems_in.at[number],
             device_id={"space": partner}, device_id_type=MESH,
         )
-
+        copy.start()
+        return copy
+
+    first = []
+    for number, y in enumerate((1 - row, row)):
+        for z in range(groups):
+            for t in range(count):
+                send_one[y, z, t] = parts[t][z, y, 1 - core].astype(jnp.bfloat16)
+        first.append(start(send_one.at[y], recv_one.at[y], number, pair))
+    first[0].wait()
+    second = []
+    for number, z in enumerate(others + [group]):
+        for t in range(count):
+            got = parts[t][z, 1 - row, core] + recv_one[1 - row, z, t].astype(jnp.float32)
+            send_two[z, t] = got.astype(jnp.bfloat16)
+        second.append(start(send_two.at[z], recv_two.at[z], 2 + number, across))
+    first[1].wait()
     for z in range(groups):
-        for y in range(2):
-            send_one[z, y] = part_ref[z, y, 1 - core].astype(jnp.bfloat16)
-    first = copy(send_one, recv_one, 0, pair)
-    first.start()
-    first.wait()
-    for z in range(groups):
-        got = part_ref[z, 1 - row, core] + recv_one[z, 1 - row].astype(jnp.float32)
-        send_two[z] = got.astype(jnp.bfloat16)
-    second = copy(send_two, recv_two, 1, across)
-    second.start()
-    for z in range(groups):
-        sum_one[z] = part_ref[z, row, core] + recv_one[z, row].astype(jnp.float32)
-    second.wait()
-    for z in range(groups):
-        sum_two[z] = sum_one[z] + recv_two[z].astype(jnp.float32)
-        send_three[z] = sum_two[z].astype(jnp.bfloat16)
-    copies = []
-    for step, other in enumerate(others):
-        copies.append(copy(send_three.at[other], recv_three.at[step], 2 + step, other * 4 + row * 2 + core))
-        copies[-1].start()
-    total = sum_two[group]
-    for step in range(groups - 1):
-        copies[step].wait()
-        total = total + recv_three[step].astype(jnp.float32)
+        for t in range(count):
+            sum_one[z, t] = parts[t][z, row, core] + recv_one[row, z, t].astype(jnp.float32)
+    third = []
+    for number, other in enumerate(others):
+        second[number].wait()
+        send_three[other] = (sum_one[other] + recv_two[other].astype(jnp.float32)).astype(jnp.bfloat16)
+        third.append(start(send_three.at[other], recv_three.at[number], 2 + groups + number, partners[number]))
+    second[-1].wait()
+    total = sum_one[group] + recv_two[group].astype(jnp.float32)
+    for number in range(groups - 1):
+        third[number].wait()
+        total = total + recv_three[number].astype(jnp.float32)
     out_ref[...] = total
 
 
-def scatter_sum(part, number):
-    devices, rows, columns = part.shape
+def scatter_sum(parts, number):
+    count = len(parts)
+    devices, rows, columns = parts[0].shape
     groups = devices // 4
     whole = pl.BlockSpec(memory_space=pltpu.VMEM)
     bf16 = jnp.bfloat16
     return pl.pallas_call(
-        functools.partial(scatter_kernel, groups),
-        out_shape=jax.ShapeDtypeStruct((rows, columns), jnp.float32),
-        in_specs=[whole],
+        functools.partial(scatter_kernel, groups, count),
+        out_shape=jax.ShapeDtypeStruct((count, rows, columns), jnp.float32),
+        in_specs=[whole] * count,
         out_specs=whole,
         scratch_shapes=[
-            pltpu.VMEM((groups, 2, rows, columns), bf16),
-            pltpu.VMEM((groups, rows, columns), bf16),
-            pltpu.VMEM((groups, rows, columns), bf16),
-            pltpu.VMEM((groups, 2, rows, columns), bf16),
-            pltpu.VMEM((groups, rows, columns), bf16),
-            pltpu.VMEM((groups, rows, columns), bf16),
-            pltpu.VMEM((groups, rows, columns), jnp.float32),
-            pltpu.VMEM((groups, rows, columns), jnp.float32),
-            pltpu.SemaphoreType.DMA((groups + 1,)),
-            pltpu.SemaphoreType.DMA((groups + 1,)),
+            pltpu.VMEM((2, groups, count, rows, columns), bf16),
+            pltpu.VMEM((groups, count, rows, columns), bf16),
+            pltpu.VMEM((groups, count, rows, columns), bf16),
+            pltpu.VMEM((2, groups, count, rows, columns), bf16),
+            pltpu.VMEM((groups, count, rows, columns), bf16),
+            pltpu.VMEM((groups, count, rows, columns), bf16),
+            pltpu.VMEM((groups, count, rows, columns), jnp.float32),
+            pltpu.SemaphoreType.DMA((2 * groups + 1,)),
+            pltpu.SemaphoreType.DMA((2 * groups + 1,)),
         ],
         compiler_params=pltpu.CompilerParams(
             collective_id=number, has_side_effects=True, vmem_limit_bytes=40 * 2**20
         ),
         name="scatter_sum",
-    )(part.reshape(groups, 2, 2, rows, columns))
+    )(*[part.reshape(groups, 2, 2, rows, columns) for part in parts])
 
 
 def by_owner(part, devices):
@@ -328,38 +332,24 @@
         (inner[None] == inner[:, None]) & (numbers[None] < numbers[:, None])
     )
     rank = jnp.sum(before.astype(jnp.int32), axis=1)
-    order = [jnp.sum(jnp.where(rank == place, numbers, 0)) for place in range(slices)]
+    order = jnp.sum(jnp.where(rank[None] == numbers[:, None], numbers[None], 0), axis=1)
     half = slices // 2
 
-    size = nev // CHUNKS
     pairs = [(source, (source - 1) % devices) for source in range(devices)]
-    above = []
-    for place in range(half):
-        for chunk in range(CHUNKS):
-            piece = lax.dynamic_slice(
-                vectors, (order[place], 0, 0, chunk * size, 0), (1, 2, 3, size, sites)
-            )
-            above.append(lax.ppermute(piece, "space", pairs)[0])
+    chosen = [lax.dynamic_slice_in_dim(vectors, order[place], 1, 0) for place in range(half)]
+    chosen, order = lax.optimization_barrier((chosen, order))
+    above = [lax.ppermute(plane, "space", pairs) for plane in chosen]
 
     links = jnp.transpose(
         link_field.reshape(slices, 3, 2, 3, 3, sites), (0, 1, 3, 4, 2, 5)
     )
-    scalars = (jnp.stack(order), directions, offsets, momentum)
+    scalars = (order, directions, offsets, momentum)
     sums_at = functools.partial(slice_sums, scalars, vectors, links, extent=extent_x, norm_factor=norm_factor)
-    results = [None] * slices
-    for place in range(half, slices):
-        part = by_owner(sums_at(None, place)[None], devices)
-        results[place] = lax.psum_scatter(part, "space", scatter_dimension=0, tiled=True)
-    for place in range(half):
-        pieces = [sums_at(above[place * CHUNKS + chunk], place) for chunk in range(CHUNKS)]
-        part = by_owner(jnp.concatenate(pieces)[None], devices)
-        if place < half - 1:
-            results[place] = lax.psum_scatter(part, "space", scatter_dimension=0, tiled=True)
-        else:
-            results[place] = scatter_sum(part, 0)[None]
+    inner_sum = scatter_sum([by_owner(sums_at(None, place)[None], devices) for place in range(half, slices)], 0)
+    outer_sum = scatter_sum([by_owner(sums_at(above[place], place)[None], devices) for place in range(half)], 1)
 
     own = nev // devices
-    both = jnp.concatenate(results).reshape(slices, 2, BLK, own, nev)
+    both = jnp.concatenate([outer_sum, inner_sum]).reshape(slices, 2, BLK, own, nev)
     return jnp.take(both, rank, axis=0, mode="clip")
 
 

time: 224 us -> 88.6 us (0.40)
  waiting for transfers between devices: 115 us -> 0.01 us
  between operations: 17 us -> 3.95 us
  local copies, waits for them, and re-layouts: 16.4 us -> 5.27 us
  Pallas kernels: 61.5 us -> 72 us
  other arithmetic: 5.81 us -> 0.98 us
    reduce_scatter x3 -> x0, waiting for transfers between devices: 115 us -> none  [on_device(): lax.psum_scatter(part, 'space', scatter_dimension=0, tiled=True)]
    pallas_call x1 -> x2, Pallas kernels: 10.4 us -> 28.7 us  [scatter_sum(): pl.pallas_call(functools.partial(scatter_kernel, groups, count), out_shap...]
    unnamed x24 -> x12, local copies, waits for them, and re-layouts: 11.4 us -> 1.04 us
    pallas_call x6 -> x4, Pallas kernels: 51 us -> 43.3 us  [slice_sums(): pl.pallas_call(functools.partial(sums_kernel, place, extent, norm_factor)...]
    another operation x2 -> x0, other arithmetic: 3.42 us -> none  [the longest x1 2.58 us: on_device(): scalars = (jnp.stack(order), directions, offsets, momentum)]
    ppermute x4 -> x2, starting transfers between devices: 7.24 us -> 6.17 us  [on_device(): above = [lax.ppermute(plane, 'space', pairs) for plane in chosen]]
  transfers between devices with their start and end apart: 7 -> 2, of which waited for: 2 -> 0; matrix products, arithmetic and copies ran while one was open for 2% -> 0% of each run, Pallas kernels for 22% -> 55%
where the time goes in v3:
time: 88.6 us; the launch traced here: 88.4 us
  Pallas kernels  72 us (81%)
  starting transfers between devices  6.17 us (7%)
  local copies, waits for them, and re-layouts  5.27 us (6%)
  between operations  3.95 us (4%)
  other arithmetic  0.98 us (1%)
    pallas_call x4, Pallas kernels, slice_sums(): pl.pallas_call(functools.partial(sums_kernel, place, extent, norm_factor)...  43.3 us
    pallas_call x2, Pallas kernels, scatter_sum(): pl.pallas_call(functools.partial(scatter_kernel, groups, count), out_shap...  28.7 us
    ppermute x2, starting transfers between devices, on_device(): above = [lax.ppermute(plane, 'space', pairs) for plane in chosen]  6.17 us
    dynamic_slice x1, local copies, waits for them, and re-layouts, on_device(): lax.dynamic_slice_in_dim(vectors, order[place], 1, 0)  2.43 us
  transfers between devices with their start and end apart: 2, of which 0 were waited for; matrix products, arithmetic and copies ran while one was open for 0% of the time, Pallas kernels for 55%

profile of v3, /device:TPU:0, one launch (start us, length us, event | category | flops | bytes accessed | tf_op | source)
XLA Modules:
  0.0 88.4 jit_solution(10890257444647582142)
XLA Ops:
  0.0 0.7 compare_convert_fusion
  0.7 0.2 convert_reduce_fusion
  0.8 0.1 select_reduce_fusion.order
  1.0 0.6 fusion.2
  5.4 0.0 copy-start
  5.4 0.0 copy-start.3
  5.4 0.0 copy-start.4
  5.4 0.0 copy-start.5
  5.4 2.4 %dynamic-slice_bitcast_fusion = (bf16[1,2,3,128,1024]{4,3,2,1,0:T(8,128)(2,1)S(1)}, bf16[1,2,3,128,1024]{4,3,2,1,0:T(8,128)(2,1)S(1)}) fusion(bf16[4,2,3,128,1,1024]{5,3,4,2,1,0:T(8,128)(2,1)} %param.5, s32[]{:T(128)S(6)} %select_n.12, s32[]{:T(128)S(6)} %select_n.11), kind=kLoop, calls=%fused_computation.1 | loop fusion | bytes 6291464 | tf_op jit(solution)/shard_map/dynamic_slice | solution.py:339
  7.8 5.5 %collective-permute-start.1 = (bf16[1,2,3,128,1024]{4,3,2,1,0:T(8,128)(2,1)S(1)}, bf16[1,2,3,128,1024]{4,3,2,1,0:T(8,128)(2,1)S(1)}, u32[]{:S(2)}, u32[]{:S(2)}) collective-permute-start(bf16[1,2,3,128,1024]{4,3,2,1,0:T(8,128)(2,1)S(1)} %get-tuple-element.10), channel_id=1, source_target_pairs={{0,15},{1,0},{2,1},{3,2},{4,3},{5,4},{6,5},{7,6},{8,7},{9,8},{10,9... | collective-permute-start | bytes 4718600 | tf_op jit(solution)/shard_map/ppermute | solution.py:341
  13.3 0.7 collective-permute-start
  14.0 0.0 copy-done
  14.0 0.0 copy-done.3
  14.0 0.0 copy-done.4
  14.0 0.0 copy-done.5
  14.0 0.0 copy-start.1
  14.0 1.0 %copy-done.1 = bf16[4,3,2,3,3,1,1024]{6,2,5,4,3,1,0:T(2,128)(2,1)S(1)} copy-done((bf16[4,3,2,3,3,1,1024]{6,2,5,4,3,1,0:T(2,128)(2,1)S(1)}, bf16[4,3,2,3,3,1,1024]{6,2,5,4,3,1,0:T(2,128)(2,1)}, u32[]{:S(2)}) %copy-start.1) | copy-done | bytes 442392
  15.0 11.2 %inner_sums.2 = f32[16,8,8,128]{3,2,1,0:T(8,128)S(1)} custom-call(s32[4]{0:T(128)S(1)} %select_reduce_fusion.order, s32[4]{0:T(128)S(1)} %copy-done.3, s32[4]{0:T(128)S(1)} %copy-done.4, s32[3]{0:T(128)S(1)} %copy-done.5, bf16[4,2,3,128,1024]{4,3,2,1,0:T(8,128)(2,1)S(1)} %bitcast.15, bf16[4,3,3,3,2,1024]{5,4,3,2,1,0:T(2,128)(2,1)S(1)} %bitcast.19), custom_call_target="tpu_custom_call" | custom-call | flops 314572800 | bytes 2097152 | tf_op jit(solution)/shard_map/inner_sums/pallas_call | solution.py:210
  26.2 0.0 copy-start.2
  26.3 11.6 %inner_sums.3 = f32[16,8,8,128]{3,2,1,0:T(8,128)S(1)} custom-call(s32[4]{0:T(128)S(1)} %select_reduce_fusion.order, s32[4]{0:T(128)S(1)} %copy-done.3, s32[4]{0:T(128)S(1)} %copy-done.4, s32[3]{0:T(128)S(1)} %copy-done.5, bf16[4,2,3,128,1024]{4,3,2,1,0:T(8,128)(2,1)S(1)} %bitcast.16, bf16[4,3,3,3,2,1024]{5,4,3,2,1,0:T(2,128)(2,1)S(1)} %bitcast.20), custom_call_target="tpu_custom_call" | custom-call | flops 314572800 | bytes 2097152 | tf_op jit(solution)/shard_map/inner_sums/pallas_call | solution.py:210
  37.9 15.9 %scatter_sum.3 = f32[2,64,128]{2,1,0:T(8,128)S(1)} custom-call(f32[4,2,2,64,128]{4,3,2,1,0:T(8,128)S(1)} %bitcast.25, f32[4,2,2,64,128]{4,3,2,1,0:T(8,128)S(1)} %bitcast.26), custom_call_target="tpu_custom_call" | custom-call | tf_op jit(solution)/shard_map/scatter_sum/pallas_call | solution.py:288
  53.8 0.0 collective-permute-done.1.refs_0_
  53.8 0.0 copy-done.2
  53.9 10.2 %outer_sums.3 = f32[16,8,8,128]{3,2,1,0:T(8,128)S(1)} custom-call(s32[4]{0:T(128)S(1)} %select_reduce_fusion.order, s32[4]{0:T(128)S(1)} %copy-done.3, s32[4]{0:T(128)S(1)} %copy-done.4, s32[3]{0:T(128)S(1)} %copy-done.5, bf16[4,2,3,128,1024]{4,3,2,1,0:T(8,128)(2,1)S(1)} %bitcast.17, bf16[4,3,3,3,2,1024]{5,4,3,2,1,0:T(2,128)(2,1)S(1)} %bitcast.21, ...), custom_call_target="tpu_custom_call" | custom-call | flops 314572800 | bytes 2097152 | tf_op jit(solution)/shard_map/outer_sums/pallas_call | solution.py:210
  64.1 0.0 collective-permute-done.refs_0_
  64.1 10.2 %outer_sums.2 = f32[16,8,8,128]{3,2,1,0:T(8,128)S(1)} custom-call(s32[4]{0:T(128)S(1)} %select_reduce_fusion.order, s32[4]{0:T(128)S(1)} %copy-done.3, s32[4]{0:T(128)S(1)} %copy-done.4, s32[3]{0:T(128)S(1)} %copy-done.5, bf16[4,2,3,128,1024]{4,3,2,1,0:T(8,128)(2,1)S(1)} %bitcast.18, bf16[4,3,3,3,2,1024]{5,4,3,2,1,0:T(2,128)(2,1)S(1)} %bitcast.22, ...), custom_call_target="tpu_custom_call" | custom-call | flops 314572800 | bytes 2097152 | tf_op jit(solution)/shard_map/outer_sums/pallas_call | solution.py:210
  74.3 12.8 %scatter_sum.2 = f32[2,64,128]{2,1,0:T(8,128)S(1)} custom-call(f32[4,2,2,64,128]{4,3,2,1,0:T(8,128)S(1)} %bitcast.24, f32[4,2,2,64,128]{4,3,2,1,0:T(8,128)S(1)} %bitcast.23), custom_call_target="tpu_custom_call" | custom-call | tf_op jit(solution)/shard_map/scatter_sum/pallas_call | solution.py:288
  87.1 1.2 %gather_fusion = f32[4,2,4,8,128]{4,3,2,1,0:T(8,128)} fusion(f32[4,2,4,8,128]{4,3,2,1,0:T(8,128)S(1)} %bitcast.27, s32[1024]{0:T(1024)S(1)} %pad_clamp_fusion), kind=kCustom, calls=%fused_computation | custom fusion | bytes 262160 | tf_op jit(solution)/shard_map/jit(_take)/gather | solution.py:353
  (2 shorter events, 0.0 us)
Async XLA Ops:
  5.4 8.7 %copy-start = (bf16[4,2,3,128,1,1024]{5,3,4,2,1,0:T(8,128)(2,1)S(1)}, bf16[4,2,3,128,1,1024]{5,3,4,2,1,0:T(8,128)(2,1)}, u32[]{:S(2)}) copy-start(bf16[4,2,3,128,1,1024]{5,3,4,2,1,0:T(8,128)(2,1)} %param.5) | copy-start | bytes 18874372
  5.4 8.7 %copy-start.3 = (s32[4]{0:T(128)S(1)}, s32[4]{0:T(128)}, u32[]{:S(2)}) copy-start(s32[4]{0:T(128)} %directions.7) | copy-start | bytes 52
  5.4 8.6 %copy-start.4 = (s32[4]{0:T(128)S(1)}, s32[4]{0:T(128)}, u32[]{:S(2)}) copy-start(s32[4]{0:T(128)} %offsets.7) | copy-start | bytes 52
  5.4 8.6 %copy-start.5 = (s32[3]{0:T(128)S(1)}, s32[3]{0:T(128)}, u32[]{:S(2)}) copy-start(s32[3]{0:T(128)} %momentum.7) | copy-start | bytes 40
  7.8 46.0 %collective-permute-start.1 = (bf16[1,2,3,128,1024]{4,3,2,1,0:T(8,128)(2,1)S(1)}, bf16[1,2,3,128,1024]{4,3,2,1,0:T(8,128)(2,1)S(1)}, u32[]{:S(2)}, u32[]{:S(2)}) collective-permute-start(bf16[1,2,3,128,1024]{4,3,2,1,0:T(8,128)(2,1)S(1)} %get-tuple-element.10), channel_id=1, source_target_pairs={{0,15},{1,0},{2,1},{3,2},{4,3},{5,4},{6,5},{7,6},{8,7},{9,8},{10,9... | collective-permute-start | bytes 4718600 | tf_op jit(solution)/shard_map/ppermute | solution.py:341
  13.3 50.8 %collective-permute-start = (bf16[1,2,3,128,1024]{4,3,2,1,0:T(8,128)(2,1)S(1)}, bf16[1,2,3,128,1024]{4,3,2,1,0:T(8,128)(2,1)S(1)}, u32[]{:S(2)}, u32[]{:S(2)}) collective-permute-start(bf16[1,2,3,128,1024]{4,3,2,1,0:T(8,128)(2,1)S(1)} %get-tuple-element.9), channel_id=1, source_target_pairs={{0,15},{1,0},{2,1},{3,2},{4,3},{5,4},{6,5},{7,6},{8,7},{9,8},{10,9... | collective-permute-start | bytes 4718600 | tf_op jit(solution)/shard_map/ppermute | solution.py:341
  14.0 1.0 %copy-start.1 = (bf16[4,3,2,3,3,1,1024]{6,2,5,4,3,1,0:T(2,128)(2,1)S(1)}, bf16[4,3,2,3,3,1,1024]{6,2,5,4,3,1,0:T(2,128)(2,1)}, u32[]{:S(2)}) copy-start(bf16[4,3,2,3,3,1,1024]{6,2,5,4,3,1,0:T(2,128)(2,1)} %param.6) | copy-start | bytes 1327108
  26.2 27.6 %copy-start.2 = (bf16[4,3,2,3,3,1,1024]{6,2,5,4,3,1,0:T(2,128)(2,1)S(1)}, bf16[4,3,2,3,3,1,1024]{6,2,5,4,3,1,0:T(2,128)(2,1)}, u32[]{:S(2)}) copy-start(bf16[4,3,2,3,3,1,1024]{6,2,5,4,3,1,0:T(2,128)(2,1)} %param.6) | copy-start | bytes 1327108

commit v4 on v3

--- a/solution.py
+++ b/solution.py
@@ -152,9 +152,52 @@
     lax.fori_loop(0, nev // ROWS, rows_step, 0)
 
 
-def sums_kernel(place, extent, norm_factor, order, directions, offsets, momentum, vec_ref, link_ref, *refs):
+def slice_at(directions, place):
+    slices = directions.shape[0]
+    inner = [jnp.where(directions[t] != 0, 1, 0) for t in range(slices)]
+    outer_count = slices - sum_of(inner)
+    seen_outer = 0
+    seen_inner = outer_count
+    found = 0
+    for t in range(slices):
+        rank = jnp.where(inner[t] == 0, seen_outer, seen_inner)
+        found = found + jnp.where(rank == place, t, 0)
+        seen_outer = seen_outer + 1 - inner[t]
+        seen_inner = seen_inner + inner[t]
+    return found
+
+
+def choose_kernel(directions, vec_ref, *refs):
+    outs, sems = refs[:-1], refs[-1]
+    copies = []
+    for place, out_ref in enumerate(outs):
+        now = slice_at(directions, place)
+        copies.append(pltpu.make_async_copy(vec_ref.at[pl.ds(now, 1)], out_ref, sems.at[place]))
+        copies[-1].start()
+    for copy in copies:
+        copy.wait()
+
+
+def choose_planes(directions, vectors, count):
+    anywhere = pl.BlockSpec(memory_space=pl.ANY)
+    return pl.pallas_call(
+        choose_kernel,
+        out_shape=[jax.ShapeDtypeStruct((1,) + vectors.shape[1:], vectors.dtype)] * count,
+        grid_spec=pltpu.PrefetchScalarGridSpec(
+            num_scalar_prefetch=1,
+            grid=(1,),
+            in_specs=[anywhere],
+            out_specs=[anywhere] * count,
+            scratch_shapes=[pltpu.SemaphoreType.DMA((count,))],
+        ),
+        compiler_params=pltpu.CompilerParams(vmem_limit_bytes=56 * 2**20),
+        name="choose_planes",
+    )(directions, vectors)
+
+
+def sums_kernel(place, extent, norm_factor, directions, offsets, momentum, vec_ref, link_ref, *refs):
     nev, sites = vec_ref.shape[3:]
-    now = order[place]
+    now = slice_at(directions, place)
     if len(refs) == 9:
         src_ref, out_ref, wide_ref, link_rows, lead_rows, weights, prod_a, prod_b, acc_ref = refs
         count = src_ref.shape[3]
@@ -188,10 +231,12 @@
     count = nev if source is None else source.shape[3]
     operands = [vectors, links] + ([] if source is None else [source])
     in_specs = [
-        pl.BlockSpec((1, 2, 3, nev, sites), lambda i, order, *_: (order[place], 0, 0, 0, 0)),
+        pl.BlockSpec((1, 2, 3, nev, sites), lambda i, directions, *_: (slice_at(directions, place), 0, 0, 0, 0)),
         pl.BlockSpec(
             (1, 1, 3, 3, 2, sites),
-            lambda i, order, directions, *_: (order[place], directions[order[place]], 0, 0, 0, 0),
+            lambda i, directions, *_: (
+                slice_at(directions, place), directions[slice_at(directions, place)], 0, 0, 0, 0
+            ),
         ),
     ]
     scratch = [
@@ -211,7 +256,7 @@
         functools.partial(sums_kernel, place, extent, norm_factor),
         out_shape=jax.ShapeDtypeStruct((count // 8, 2 * BLK, 8, nev), jnp.float32),
         grid_spec=pltpu.PrefetchScalarGridSpec(
-            num_scalar_prefetch=4,
+            num_scalar_prefetch=3,
             grid=(1,),
             in_specs=in_specs,
             out_specs=pl.BlockSpec((count // 8, 2 * BLK, 8, nev), lambda i, *_: (0, 0, 0, 0)),
@@ -332,24 +377,24 @@
         (inner[None] == inner[:, None]) & (numbers[None] < numbers[:, None])
     )
     rank = jnp.sum(before.astype(jnp.int32), axis=1)
-    order = jnp.sum(jnp.where(rank[None] == numbers[:, None], numbers[None], 0), axis=1)
     half = slices // 2
 
     pairs = [(source, (source - 1) % devices) for source in range(devices)]
-    chosen = [lax.dynamic_slice_in_dim(vectors, order[place], 1, 0) for place in range(half)]
-    chosen, order = lax.optimization_barrier((chosen, order))
+    chosen = choose_planes(directions, vectors, half)
+    chosen, turned = lax.optimization_barrier((chosen, directions))
     above = [lax.ppermute(plane, "space", pairs) for plane in chosen]
 
     links = jnp.transpose(
         link_field.reshape(slices, 3, 2, 3, 3, sites), (0, 1, 3, 4, 2, 5)
     )
-    scalars = (order, directions, offsets, momentum)
+    scalars = (turned, offsets, momentum)
     sums_at = functools.partial(slice_sums, scalars, vectors, links, extent=extent_x, norm_factor=norm_factor)
-    inner_sum = scatter_sum([by_owner(sums_at(None, place)[None], devices) for place in range(half, slices)], 0)
-    outer_sum = scatter_sum([by_owner(sums_at(above[place], place)[None], devices) for place in range(half)], 1)
+    inner = [by_owner(sums_at(None, place)[None], devices) for place in range(half, slices)]
+    outer = [by_owner(sums_at(above[place], place)[None], devices) for place in range(half)]
+    sums = scatter_sum(outer + inner, 0)
 
     own = nev // devices
-    both = jnp.concatenate([outer_sum, inner_sum]).reshape(slices, 2, BLK, own, nev)
+    both = sums.reshape(slices, 2, BLK, own, nev)
     return jnp.take(both, rank, axis=0, mode="clip")
 
 

time: 88.6 us -> 165 us (1.86)
  Pallas kernels: 72 us -> 156 us
  between operations: 3.95 us -> 0.08 us
  local copies, waits for them, and re-layouts: 5.27 us -> 2.23 us
    pallas_call x0 -> x1, Pallas kernels: none -> 97.2 us  [choose_planes(): pl.pallas_call(choose_kernel, out_shape=[jax.ShapeDtypeStruct((1,) + vect...]
    pallas_call x2 -> x1, Pallas kernels: 28.7 us -> 15.6 us  [scatter_sum(): pl.pallas_call(functools.partial(scatter_kernel, groups, count), out_shap...]
    dynamic_slice x1 -> x0, local copies, waits for them, and re-layouts: 2.43 us -> none  [on_device(): lax.dynamic_slice_in_dim(vectors, order[place], 1, 0)]
  transfers between devices with their start and end apart: 2 -> 2, of which waited for: 0 -> 1; matrix products, arithmetic and copies ran while one was open for 0% -> 0% of each run, Pallas kernels for 55% -> 20%
where the time goes in v4:
time: 165 us
  Pallas kernels  156 us (95%)
  starting transfers between devices  6.18 us (4%)
  local copies, waits for them, and re-layouts  2.23 us (1%)
    pallas_call x1, Pallas kernels, choose_planes(): pl.pallas_call(choose_kernel, out_shape=[jax.ShapeDtypeStruct((1,) + vect...  97.2 us
    pallas_call x4, Pallas kernels, slice_sums(): pl.pallas_call(functools.partial(sums_kernel, place, extent, norm_factor)...  43.3 us
    pallas_call x1, Pallas kernels, scatter_sum(): pl.pallas_call(functools.partial(scatter_kernel, groups, count), out_shap...  15.6 us
    ppermute x2, starting transfers between devices, on_device(): above = [lax.ppermute(plane, 'space', pairs) for plane in chosen]  6.18 us
  transfers between devices with their start and end apart: 2, of which 1 were waited for; matrix products, arithmetic and copies ran while one was open for 0% of the time, Pallas kernels for 20%

profile of v4, /device:TPU:0, one launch (start us, length us, event | category | flops | bytes accessed | tf_op | source)
XLA Modules:
  0.0 164.9 jit_solution(7264452919233804470)
XLA Ops:
  0.0 0.0 copy-start
  0.0 0.0 copy-start.2
  0.0 0.0 copy-start.3
  0.0 0.0 copy-start.4
  0.0 97.2 %choose_planes.1 = (bf16[1,2,3,128,1024]{4,3,2,1,0:T(8,128)(2,1)}, bf16[1,2,3,128,1024]{4,3,2,1,0:T(8,128)(2,1)}) custom-call(s32[4]{0:T(128)} %directions.5, bf16[4,2,3,128,1024]{4,3,2,1,0:T(8,128)(2,1)} %bitcast.9), custom_call_target="tpu_custom_call" | custom-call | tf_op jit(solution)/shard_map/choose_planes/pallas_call | solution.py:183
  97.2 5.5 %collective-permute-start.1 = (bf16[1,2,3,128,1024]{4,3,2,1,0:T(8,128)(2,1)}, bf16[1,2,3,128,1024]{4,3,2,1,0:T(8,128)(2,1)S(1)}, u32[]{:S(2)}, u32[]{:S(2)}) collective-permute-start(bf16[1,2,3,128,1024]{4,3,2,1,0:T(8,128)(2,1)} %get-tuple-element.14), channel_id=1, source_target_pairs={{0,15},{1,0},{2,1},{3,2},{4,3},{5,4},{6,5},{7,6},{8,7},{9,8},{10,9... | collective-permute-start | bytes 4718600 | tf_op jit(solution)/shard_map/ppermute | solution.py:385
  102.7 0.7 collective-permute-start
  103.4 0.0 copy-done
  103.4 0.0 copy-done.2
  103.4 0.0 copy-done.3
  103.4 0.0 copy-done.4
  103.4 0.0 copy-start.1
  103.4 1.0 copy-done.1
  104.5 11.2 %inner_sums.2 = f32[16,8,8,128]{3,2,1,0:T(8,128)S(1)} custom-call(s32[4]{0:T(128)S(1)} %copy-done.2, s32[4]{0:T(128)S(1)} %copy-done.3, s32[3]{0:T(128)S(1)} %copy-done.4, bf16[4,2,3,128,1024]{4,3,2,1,0:T(8,128)(2,1)S(1)} %bitcast.10, bf16[4,3,3,3,2,1024]{5,4,3,2,1,0:T(2,128)(2,1)S(1)} %bitcast.14), custom_call_target="tpu_custom_call" | custom-call | flops 314572800 | bytes 2097152 | tf_op jit(solution)/shard_map/inner_sums/pallas_call | solution.py:255
  115.7 11.6 %inner_sums.3 = f32[16,8,8,128]{3,2,1,0:T(8,128)S(1)} custom-call(s32[4]{0:T(128)S(1)} %copy-done.2, s32[4]{0:T(128)S(1)} %copy-done.3, s32[3]{0:T(128)S(1)} %copy-done.4, bf16[4,2,3,128,1024]{4,3,2,1,0:T(8,128)(2,1)S(1)} %bitcast.11, bf16[4,3,3,3,2,1024]{5,4,3,2,1,0:T(2,128)(2,1)S(1)} %bitcast.15), custom_call_target="tpu_custom_call" | custom-call | flops 314572800 | bytes 2097152 | tf_op jit(solution)/shard_map/inner_sums/pallas_call | solution.py:255
  127.3 0.2 convert_reduce_fusion
  127.5 0.0 collective-permute-done.1.refs_0_
  127.5 10.2 %outer_sums.3 = f32[16,8,8,128]{3,2,1,0:T(8,128)S(1)} custom-call(s32[4]{0:T(128)S(1)} %copy-done.2, s32[4]{0:T(128)S(1)} %copy-done.3, s32[3]{0:T(128)S(1)} %copy-done.4, bf16[4,2,3,128,1024]{4,3,2,1,0:T(8,128)(2,1)S(1)} %bitcast.12, bf16[4,3,3,3,2,1024]{5,4,3,2,1,0:T(2,128)(2,1)S(1)} %bitcast.16, ...), custom_call_target="tpu_custom_call" | custom-call | flops 314572800 | bytes 2097152 | tf_op jit(solution)/shard_map/outer_sums/pallas_call | solution.py:255
  137.7 0.1 collective-permute-done.refs_0_
  137.8 10.2 %outer_sums.2 = f32[16,8,8,128]{3,2,1,0:T(8,128)S(1)} custom-call(s32[4]{0:T(128)S(1)} %copy-done.2, s32[4]{0:T(128)S(1)} %copy-done.3, s32[3]{0:T(128)S(1)} %copy-done.4, bf16[4,2,3,128,1024]{4,3,2,1,0:T(8,128)(2,1)S(1)} %bitcast.13, bf16[4,3,3,3,2,1024]{5,4,3,2,1,0:T(2,128)(2,1)S(1)} %bitcast.17, bf16[1,2,3,128,1024]{4,3,2,1,0:T(8,128)(2,1)S(1)} %collective-permute-done.refs_0_), custom_call_target="tpu_custom_call" | custom-call | flops 314572800 | bytes 2097152 | tf_op jit(solution)/shard_map/outer_sums/pallas_call | solution.py:255
  148.1 15.6 %scatter_sum.1 = f32[4,64,128]{2,1,0:T(8,128)S(1)} custom-call(f32[4,2,2,64,128]{4,3,2,1,0:T(8,128)S(1)} %bitcast.19, f32[4,2,2,64,128]{4,3,2,1,0:T(8,128)S(1)} %bitcast.18, f32[4,2,2,64,128]{4,3,2,1,0:T(8,128)S(1)} %bitcast.20, f32[4,2,2,64,128]{4,3,2,1,0:T(8,128)S(1)} %bitcast.21), custom_call_target="tpu_custom_call" | custom-call | tf_op jit(solution)/shard_map/scatter_sum/pallas_call | solution.py:333
  163.6 1.2 gather_fusion
  (2 shorter events, 0.0 us)
Async XLA Ops:
  0.0 103.4 %copy-start = (bf16[4,2,3,128,1,1024]{5,3,4,2,1,0:T(8,128)(2,1)S(1)}, bf16[4,2,3,128,1,1024]{5,3,4,2,1,0:T(8,128)(2,1)}, u32[]{:S(2)}) copy-start(bf16[4,2,3,128,1,1024]{5,3,4,2,1,0:T(8,128)(2,1)} %param.5) | copy-start | bytes 18874372
  0.0 103.4 %copy-start.2 = (s32[4]{0:T(128)S(1)}, s32[4]{0:T(128)}, u32[]{:S(2)}) copy-start(s32[4]{0:T(128)} %directions.5) | copy-start | bytes 52
  0.0 103.4 %copy-start.3 = (s32[4]{0:T(128)S(1)}, s32[4]{0:T(128)}, u32[]{:S(2)}) copy-start(s32[4]{0:T(128)} %offsets.7) | copy-start | bytes 52
  0.0 103.4 %copy-start.4 = (s32[3]{0:T(128)S(1)}, s32[3]{0:T(128)}, u32[]{:S(2)}) copy-start(s32[3]{0:T(128)} %momentum.7) | copy-start | bytes 40
  97.2 30.3 %collective-permute-start.1 = (bf16[1,2,3,128,1024]{4,3,2,1,0:T(8,128)(2,1)}, bf16[1,2,3,128,1024]{4,3,2,1,0:T(8,128)(2,1)S(1)}, u32[]{:S(2)}, u32[]{:S(2)}) collective-permute-start(bf16[1,2,3,128,1024]{4,3,2,1,0:T(8,128)(2,1)} %get-tuple-element.14), channel_id=1, source_target_pairs={{0,15},{1,0},{2,1},{3,2},{4,3},{5,4},{6,5},{7,6},{8,7},{9,8},{10,9... | collective-permute-start | bytes 4718600 | tf_op jit(solution)/shard_map/ppermute | solution.py:385
  102.7 35.1 %collective-permute-start = (bf16[1,2,3,128,1024]{4,3,2,1,0:T(8,128)(2,1)}, bf16[1,2,3,128,1024]{4,3,2,1,0:T(8,128)(2,1)S(1)}, u32[]{:S(2)}, u32[]{:S(2)}) collective-permute-start(bf16[1,2,3,128,1024]{4,3,2,1,0:T(8,128)(2,1)} %get-tuple-element.13), channel_id=1, source_target_pairs={{0,15},{1,0},{2,1},{3,2},{4,3},{5,4},{6,5},{7,6},{8,7},{9,8},{10,9... | collective-permute-start | bytes 4718600 | tf_op jit(solution)/shard_map/ppermute | solution.py:385
  103.4 1.0 copy-start.1

commit v5 on v4

--- a/solution.py
+++ b/solution.py
@@ -167,32 +167,32 @@
     return found
 
 
-def choose_kernel(directions, vec_ref, *refs):
-    outs, sems = refs[:-1], refs[-1]
-    copies = []
-    for place, out_ref in enumerate(outs):
-        now = slice_at(directions, place)
-        copies.append(pltpu.make_async_copy(vec_ref.at[pl.ds(now, 1)], out_ref, sems.at[place]))
-        copies[-1].start()
-    for copy in copies:
-        copy.wait()
+def choose_kernel(directions, *refs):
+    count = len(refs) // 2
+    for place in range(count):
+        refs[count + place][...] = refs[place][...]
 
 
 def choose_planes(directions, vectors, count):
-    anywhere = pl.BlockSpec(memory_space=pl.ANY)
+    _, _, colors, nev, sites = vectors.shape
+
+    def block(place):
+        return pl.BlockSpec(
+            (1, 2, 1, nev, sites), lambda c, directions: (slice_at(directions, place), 0, c, 0, 0)
+        )
+
     return pl.pallas_call(
         choose_kernel,
         out_shape=[jax.ShapeDtypeStruct((1,) + vectors.shape[1:], vectors.dtype)] * count,
         grid_spec=pltpu.PrefetchScalarGridSpec(
             num_scalar_prefetch=1,
-            grid=(1,),
-            in_specs=[anywhere],
-            out_specs=[anywhere] * count,
-            scratch_shapes=[pltpu.SemaphoreType.DMA((count,))],
+            grid=(colors,),
+            in_specs=[block(place) for place in range(count)],
+            out_specs=[pl.BlockSpec((1, 2, 1, nev, sites), lambda c, directions: (0, 0, c, 0, 0))] * count,
         ),
         compiler_params=pltpu.CompilerParams(vmem_limit_bytes=56 * 2**20),
         name="choose_planes",
-    )(directions, vectors)
+    )(directions, *[vectors] * count)
 
 
 def sums_kernel(place, extent, norm_factor, directions, offsets, momentum, vec_ref, link_ref, *refs):

time: 165 us -> 73.4 us (0.44)
  Pallas kernels: 156 us -> 64.5 us
    pallas_call x1, Pallas kernels: 97.2 us -> 5.7 us  [choose_planes(): pl.pallas_call(choose_kernel, out_shape=[jax.ShapeDtypeStruct((1,) + vect...]
  transfers between devices with their start and end apart: 2 -> 2, of which waited for: 1 -> 1; matrix products, arithmetic and copies ran while one was open for 0% -> 0% of each run, Pallas kernels for 20% -> 45%
where the time goes in v5:
time: 73.4 us; the launch traced here: 73.3 us
  Pallas kernels  64.5 us (88%)
  starting transfers between devices  6.12 us (8%)
  local copies, waits for them, and re-layouts  1.23 us (2%)
  waiting for transfers between devices  1.09 us (1%)
    pallas_call x4, Pallas kernels, slice_sums(): pl.pallas_call(functools.partial(sums_kernel, place, extent, norm_factor)...  43.3 us
    pallas_call x1, Pallas kernels, scatter_sum(): pl.pallas_call(functools.partial(scatter_kernel, groups, count), out_shap...  15.6 us
    ppermute x2, starting transfers between devices, on_device(): above = [lax.ppermute(plane, 'space', pairs) for plane in chosen]  6.12 us
    pallas_call x1, Pallas kernels, choose_planes(): pl.pallas_call(choose_kernel, out_shape=[jax.ShapeDtypeStruct((1,) + vect...  5.7 us
  transfers between devices with their start and end apart: 2, of which 1 were waited for; matrix products, arithmetic and copies ran while one was open for 0% of the time, Pallas kernels for 45%

profile of v5, /device:TPU:0, one launch (start us, length us, event | category | flops | bytes accessed | tf_op | source)
XLA Modules:
  0.0 73.3 jit_solution(14715377399723052339)
XLA Ops:
  0.0 0.0 slice-start
  0.0 0.0 slice-start.1
  0.0 0.0 copy-start
  0.0 0.0 copy-start.1
  0.0 0.0 copy-start.2
  0.0 0.0 copy-start.3
  0.0 5.7 %choose_planes.1 = (bf16[1,2,3,128,1024]{4,3,2,1,0:T(8,128)(2,1)}, bf16[1,2,3,128,1024]{4,3,2,1,0:T(8,128)(2,1)}) custom-call(s32[4]{0:T(128)} %directions.5, bf16[4,2,3,128,1024]{4,3,2,1,0:T(8,128)(2,1)} %bitcast.9, bf16[4,2,3,128,1024]{4,3,2,1,0:T(8,128)(2,1)} %bitcast.10), custom_call_target="tpu_custom_call" | custom-call | tf_op jit(solution)/shard_map/choose_planes/pallas_call | solution.py:184
  5.7 5.4 %collective-permute-start.1 = (bf16[1,2,3,128,1024]{4,3,2,1,0:T(8,128)(2,1)}, bf16[1,2,3,128,1024]{4,3,2,1,0:T(8,128)(2,1)S(1)}, u32[]{:S(2)}, u32[]{:S(2)}) collective-permute-start(bf16[1,2,3,128,1024]{4,3,2,1,0:T(8,128)(2,1)} %get-tuple-element.14), channel_id=1, source_target_pairs={{0,15},{1,0},{2,1},{3,2},{4,3},{5,4},{6,5},{7,6},{8,7},{9,8},{10,9... | collective-permute-start | bytes 4718600 | tf_op jit(solution)/shard_map/ppermute | solution.py:385
  11.2 0.7 collective-permute-start
  11.8 0.0 slice-done
  11.8 0.0 slice-done.1
  11.8 0.0 copy-done
  11.9 0.0 copy-done.1
  11.9 0.0 copy-done.2
  11.9 0.0 copy-done.3
  11.9 11.2 %inner_sums.2 = f32[16,8,8,128]{3,2,1,0:T(8,128)S(1)} custom-call(s32[4]{0:T(128)S(1)} %copy-done.1, s32[4]{0:T(128)S(1)} %copy-done.2, s32[3]{0:T(128)S(1)} %copy-done.3, bf16[4,2,3,128,1024]{4,3,2,1,0:T(8,128)(2,1)S(1)} %bitcast.13, bf16[4,3,3,3,2,1024]{5,4,3,2,1,0:T(2,128)(2,1)S(1)} %bitcast.17), custom_call_target="tpu_custom_call" | custom-call | flops 314572800 | bytes 2097152 | tf_op jit(solution)/shard_map/inner_sums/pallas_call | solution.py:255
  23.1 11.6 %inner_sums.3 = f32[16,8,8,128]{3,2,1,0:T(8,128)S(1)} custom-call(s32[4]{0:T(128)S(1)} %copy-done.1, s32[4]{0:T(128)S(1)} %copy-done.2, s32[3]{0:T(128)S(1)} %copy-done.3, bf16[4,2,3,128,1024]{4,3,2,1,0:T(8,128)(2,1)S(1)} %bitcast.14, bf16[4,3,3,3,2,1024]{5,4,3,2,1,0:T(2,128)(2,1)S(1)} %bitcast.18), custom_call_target="tpu_custom_call" | custom-call | flops 314572800 | bytes 2097152 | tf_op jit(solution)/shard_map/inner_sums/pallas_call | solution.py:255
  34.7 0.2 convert_reduce_fusion
  34.9 0.0 collective-permute-done.1.refs_0_
  34.9 10.2 %outer_sums.3 = f32[16,8,8,128]{3,2,1,0:T(8,128)S(1)} custom-call(s32[4]{0:T(128)S(1)} %copy-done.1, s32[4]{0:T(128)S(1)} %copy-done.2, s32[3]{0:T(128)S(1)} %copy-done.3, bf16[4,2,3,128,1024]{4,3,2,1,0:T(8,128)(2,1)S(1)} %bitcast.15, bf16[4,3,3,3,2,1024]{5,4,3,2,1,0:T(2,128)(2,1)S(1)} %bitcast.19, ...), custom_call_target="tpu_custom_call" | custom-call | flops 314572800 | bytes 2097152 | tf_op jit(solution)/shard_map/outer_sums/pallas_call | solution.py:255
  45.2 1.1 %collective-permute-done.refs_0_ = bf16[1,2,3,128,1024]{4,3,2,1,0:T(8,128)(2,1)S(1)} collective-permute-done((bf16[1,2,3,128,1024]{4,3,2,1,0:T(8,128)(2,1)}, bf16[1,2,3,128,1024]{4,3,2,1,0:T(8,128)(2,1)S(1)}, u32[]{:S(2)}, u32[]{:S(2)}) %collective-permute-start) | collective-permute-done | bytes 1572896 | tf_op jit(solution)/shard_map/ppermute | solution.py:385
  46.3 10.2 %outer_sums.2 = f32[16,8,8,128]{3,2,1,0:T(8,128)S(1)} custom-call(s32[4]{0:T(128)S(1)} %copy-done.1, s32[4]{0:T(128)S(1)} %copy-done.2, s32[3]{0:T(128)S(1)} %copy-done.3, bf16[4,2,3,128,1024]{4,3,2,1,0:T(8,128)(2,1)S(1)} %bitcast.16, bf16[4,3,3,3,2,1024]{5,4,3,2,1,0:T(2,128)(2,1)S(1)} %bitcast.20, bf16[1,2,3,128,1024]{4,3,2,1,0:T(8,128)(2,1)S(1)} %collective-permute-done.refs_0_), custom_call_target="tpu_custom_call" | custom-call | flops 314572800 | bytes 2097152 | tf_op jit(solution)/shard_map/outer_sums/pallas_call | solution.py:255
  56.5 15.6 %scatter_sum.1 = f32[4,64,128]{2,1,0:T(8,128)S(1)} custom-call(f32[4,2,2,64,128]{4,3,2,1,0:T(8,128)S(1)} %bitcast.22, f32[4,2,2,64,128]{4,3,2,1,0:T(8,128)S(1)} %bitcast.21, f32[4,2,2,64,128]{4,3,2,1,0:T(8,128)S(1)} %bitcast.23, f32[4,2,2,64,128]{4,3,2,1,0:T(8,128)S(1)} %bitcast.24), custom_call_target="tpu_custom_call" | custom-call | tf_op jit(solution)/shard_map/scatter_sum/pallas_call | solution.py:333
  72.1 1.2 %gather_fusion = f32[4,2,4,8,128]{4,3,2,1,0:T(8,128)} fusion(f32[4,2,4,8,128]{4,3,2,1,0:T(8,128)S(1)} %bitcast.25, s32[1024]{0:T(1024)S(1)} %pad_clamp_fusion), kind=kCustom, calls=%fused_computation | custom fusion | bytes 262160 | tf_op jit(solution)/shard_map/jit(_take)/gather | solution.py:398
  (3 shorter events, 0.0 us)
Async XLA Ops:
  0.0 11.8 %slice-start = ((s8[6291456]{0:T(1024)(128)(4,1)}), s8[4194304]{0:T(1024)(128)(4,1)S(1)}, s32[]{:S(2)}) async-start(s8[6291456]{0:T(1024)(128)(4,1)} %bitcast.11), calls=%async_computation | async-start | bytes 8388608
  0.0 11.8 %slice-start.1 = ((s8[6291456]{0:T(1024)(128)(4,1)}), s8[2097152]{0:T(1024)(128)(4,1)S(1)}, s32[]{:S(2)}) async-start(s8[6291456]{0:T(1024)(128)(4,1)} %bitcast.11), calls=%async_computation.1 | async-start | bytes 4194304
  0.0 11.8 %copy-start = (bf16[4,3,2,3,3,1,1024]{6,2,5,4,3,1,0:T(2,128)(2,1)S(1)}, bf16[4,3,2,3,3,1,1024]{6,2,5,4,3,1,0:T(2,128)(2,1)}, u32[]{:S(2)}) copy-start(bf16[4,3,2,3,3,1,1024]{6,2,5,4,3,1,0:T(2,128)(2,1)} %param.6) | copy-start | bytes 1327108
  0.0 11.8 %copy-start.1 = (s32[4]{0:T(128)S(1)}, s32[4]{0:T(128)}, u32[]{:S(2)}) copy-start(s32[4]{0:T(128)} %directions.5) | copy-start | bytes 52
  0.0 11.8 %copy-start.2 = (s32[4]{0:T(128)S(1)}, s32[4]{0:T(128)}, u32[]{:S(2)}) copy-start(s32[4]{0:T(128)} %offsets.7) | copy-start | bytes 52
  0.0 11.9 %copy-start.3 = (s32[3]{0:T(128)S(1)}, s32[3]{0:T(128)}, u32[]{:S(2)}) copy-start(s32[3]{0:T(128)} %momentum.7) | copy-start | bytes 40
  5.7 29.2 %collective-permute-start.1 = (bf16[1,2,3,128,1024]{4,3,2,1,0:T(8,128)(2,1)}, bf16[1,2,3,128,1024]{4,3,2,1,0:T(8,128)(2,1)S(1)}, u32[]{:S(2)}, u32[]{:S(2)}) collective-permute-start(bf16[1,2,3,128,1024]{4,3,2,1,0:T(8,128)(2,1)} %get-tuple-element.14), channel_id=1, source_target_pairs={{0,15},{1,0},{2,1},{3,2},{4,3},{5,4},{6,5},{7,6},{8,7},{9,8},{10,9... | collective-permute-start | bytes 4718600 | tf_op jit(solution)/shard_map/ppermute | solution.py:385
  11.2 35.1 %collective-permute-start = (bf16[1,2,3,128,1024]{4,3,2,1,0:T(8,128)(2,1)}, bf16[1,2,3,128,1024]{4,3,2,1,0:T(8,128)(2,1)S(1)}, u32[]{:S(2)}, u32[]{:S(2)}) collective-permute-start(bf16[1,2,3,128,1024]{4,3,2,1,0:T(8,128)(2,1)} %get-tuple-element.13), channel_id=1, source_target_pairs={{0,15},{1,0},{2,1},{3,2},{4,3},{5,4},{6,5},{7,6},{8,7},{9,8},{10,9... | collective-permute-start | bytes 4718600 | tf_op jit(solution)/shard_map/ppermute | solution.py:385
